TPU v7x, 32 devices: a whole 2x2x4 slice. The times are simulated.
32 devices in a mesh: cross: 2 (over core), strike: 16 (over z, y, x).
Axes of the slice: x: 2, y: 2, z: 4, core: 2. Of those that a mesh axis runs over, the one named last changes fastest.
Arguments:
- pressure: float32 [1024, 2, 2048], P('strike', 'cross'), may hold values from -6 to 6
- source: float32 [1024, 2, 2048], P('strike', 'cross'), may hold values from -6 to 6
- facies: int32 [1024, 2, 2048], P('strike', 'cross'), may hold values from 0 to 7
- mobility_table: float32 [8], replicated, may hold values from 0.3 to 3
Outputs:
- pressure_out: float32 [1024, 2, 2048], P('strike', 'cross')
- defect: float32 [1024, 2, 2048], P('strike', 'cross')
All inputs are finite; a program needn't handle non-finite values.
Results may differ from a plain program's by a relative error of at most 0.0003.
Values sent between devices are 32-bit elements; how exact they have to be, the bound alone decides.
A program may use at most 64 MiB of HBM per device.

v0:
```python
import math

import jax
import jax.numpy as jnp
from jax import lax
from jax.sharding import PartitionSpec as P

ND = 1024
CLASSES = 8
DEFECT = 2
SWEEPS = 3


STORE = 0.5
LOW = 0.05
HIGH = 1.95


def extended(cells, sides, width):
    for axis, dim in sides:
        count = lax.axis_size(axis)
        ends = count - 1
        head = lax.slice_in_dim(cells, 0, width, axis=dim)
        tail = lax.slice_in_dim(cells, cells.shape[dim] - width, cells.shape[dim], axis=dim)
        cells = jnp.concatenate(
            [
                lax.ppermute(tail, axis, [(i, (i + 1) % count) for i in range(ends)]),
                cells,
                lax.ppermute(head, axis, [((i + 1) % count, i) for i in range(ends)]),
            ],
            axis=dim,
        )
    return cells


def chebyshev_weights(count):
    middle = 0.5 * (LOW + HIGH)
    half = 0.5 * (HIGH - LOW)
    return [
        1.0 / (middle + half * math.cos(math.pi * (2 * j + 1) / (2 * count))) for j in range(count)
    ]


def neighbour(padded, axis, offset, shape):
    starts = [1, 1, 1]
    starts[axis] = offset
    limits = [s + n for s, n in zip(starts, shape)]
    return lax.slice(padded, starts, limits)


def operate_padded(field, mobile, padded_f, padded_m):
    total = STORE * field
    for axis in range(3):
        for offset in (0, 2):
            near_f = neighbour(padded_f, axis, offset, field.shape)
            near_m = neighbour(padded_m, axis, offset, field.shape)
            total = total + 0.5 * (mobile + near_m) * (field - near_f)
    return total


def lookup(classes, table):
    base = jnp.zeros(classes.shape, jnp.float32)
    for code in range(CLASSES):
        base = jnp.where(classes == code, table[code], base)
    return base


def cosine_table():
    index = jnp.arange(ND, dtype=jnp.int32)
    phase = index[:, None] * (2 * index[None, :] + 1) % (4 * ND)
    scale = jnp.where(index == 0, math.sqrt(1.0 / ND), math.sqrt(2.0 / ND)).astype(jnp.float32)
    return scale[:, None] * jnp.cos(phase.astype(jnp.float32) * (math.pi / (2 * ND)))


def apply_table(matrix, field):
    flat = field.reshape(field.shape[0], -1)
    product = jnp.dot(
        matrix, flat, precision=lax.Precision.HIGHEST, preferred_element_type=jnp.float32
    )
    return product.reshape(field.shape)


def plane_sweeps(rhat, mref):
    omega = chebyshev_weights(SWEEPS)
    wave = jnp.arange(ND, dtype=jnp.int32).astype(jnp.float32)
    lam = (2.0 - 2.0 * jnp.cos(wave * (math.pi / ND)))[:, None, None]
    diag = STORE + mref * (lam + 4.0)
    answer = omega[0] * rhat / diag
    for step in range(1, SWEEPS):
        padded = extended(answer, (("cross", 1), ("strike", 2)), 1)
        near = (
            padded[:, :-2, 1:-1] + padded[:, 2:, 1:-1] + padded[:, 1:-1, :-2] + padded[:, 1:-1, 2:]
        )
        answer = answer + omega[step] * (rhat - (diag * answer - mref * near)) / diag
    return answer


def per_device(pressure, source, facies, mobility_table):
    table = cosine_table()
    inverse = table.T
    base = lookup(facies, mobility_table)
    field, load, base_cols = (
        lax.all_to_all(pressure, "strike", split_axis=2, concat_axis=0, tiled=True),
        lax.all_to_all(source, "strike", split_axis=2, concat_axis=0, tiled=True),
        lax.all_to_all(base, "strike", split_axis=2, concat_axis=0, tiled=True),
    )
    defect = jnp.zeros_like(field)
    for step in range(DEFECT):
        mobile = base_cols * (1.0 + 0.5 * jnp.tanh(field))
        stacked = jnp.stack([field, mobile])
        rims = extended(stacked, (("cross", 2), ("strike", 3)), 1)
        rims = jnp.pad(rims, ((0, 0), (1, 1), (0, 0), (0, 0)))
        residual = load - operate_padded(field, mobile, rims[0], rims[1])
        defect = residual
        rhat = apply_table(table, residual)
        mref = jnp.mean(mobile, axis=0, keepdims=True)
        answer = plane_sweeps(rhat, mref)
        field = field + apply_table(inverse, answer)
    return (
        lax.all_to_all(field, "strike", split_axis=0, concat_axis=2, tiled=True),
        lax.all_to_all(defect, "strike", split_axis=0, concat_axis=2, tiled=True),
    )


def solution(mesh):
    in_specs = (
        P("strike", "cross", None),
        P("strike", "cross", None),
        P("strike", "cross", None),
        P(),
    )
    out_specs = (P("strike", "cross", None), P("strike", "cross", None))
    return jax.shard_map(
        per_device, mesh=mesh, in_specs=in_specs, out_specs=out_specs, check_vma=False
    )
```

profile of v0, /device:TPU:0, one launch (start us, length us, event | category | flops | bytes accessed | tf_op | source)
XLA Modules:
  0.0 336.1 jit_solution(1067911407493326314)
XLA Ops:
  0.6 1.6 fusion.158
  2.3 2.2 copy.118
  4.5 9.6 %fusion.159 = f32[2048,1,64]{2,1,0:T(1,128)S(1)} fusion(f32[]{:T(128)} %bitcast.15, s32[64,1,2048]{0,1,2:T(1,128)S(1)} %copy.118, f32[]{:T(128)} %bitcast.14, f32[]{:T(128)} %bitcast.13, f32[]{:T(128)} %bitcast.12, f32[]{:T(128)} %bitcast.11, f32[]{:T(128)} %bitcast.10, f32[]{:T(128)} %bitcast.9, f32[]{:T(128)} %bitcast.8), kind=kLoop, calls=%fused_computation.244 | loop fusion | flops 2097152 | bytes 1048608
  14.7 9.4 %reduce.8 = f32[2048,64]{1,0:T(8,128)S(1)} reduce(f32[2048,1,64]{2,1,0:T(1,128)S(1)} %fusion.159, f32[]{:T(128)} %broadcast.346), dimensions={1}, to_apply=%fusion.159.reduce_sub_computation | reduce | bytes 1048580
  24.1 1.4 reshape.255
  25.5 8.3 %all-to-all-start.2 = ((f32[16,1,8192]{2,1,0:T(1,128)}), f32[16,1,8192]{2,1,0:T(1,128)S(1)}, u32[]{:S(2)}, u32[]{:S(2)}) async-start(f32[16,1,8192]{2,1,0:T(1,128)} %reshape.255), calls=%async_computation.2 | async-start | bytes 1048576 | tf_op jit(solution)/shard_map/all_to_all | solution.py:105
  34.5 9.4 %reduce.4 = f32[2048,64]{1,0:T(8,128)S(1)} reduce(f32[2048,1,64]{2,1,0:T(1,128)S(1)} %bitcast.103, f32[]{:T(128)} %broadcast.346), dimensions={1}, to_apply=%bitcast.83.reduce_sub_computation | reduce | bytes 1048580
  43.9 1.4 reshape.251
  45.4 3.6 %all-to-all-done.2 = f32[16,1,8192]{2,1,0:T(1,128)S(1)} async-done(((f32[16,1,8192]{2,1,0:T(1,128)}), f32[16,1,8192]{2,1,0:T(1,128)S(1)}, u32[]{:S(2)}, u32[]{:S(2)}) %all-to-all-start.2) | async-done | bytes 524320 | tf_op jit(solution)/shard_map/all_to_all | solution.py:105
  49.0 15.4 %all-to-all-start = ((f32[16,1,8192]{2,1,0:T(1,128)}), f32[16,1,8192]{2,1,0:T(1,128)S(1)}, u32[]{:S(2)}, u32[]{:S(2)}) async-start(f32[16,1,8192]{2,1,0:T(1,128)} %reshape.251), calls=%async_computation | async-start | bytes 1048576 | tf_op jit(solution)/shard_map/all_to_all | solution.py:103
  64.4 1.9 reduce.9
  66.3 1.3 reshape.256
  69.5 9.3 %all-to-all-done = f32[16,1,8192]{2,1,0:T(1,128)S(1)} async-done(((f32[16,1,8192]{2,1,0:T(1,128)}), f32[16,1,8192]{2,1,0:T(1,128)S(1)}, u32[]{:S(2)}, u32[]{:S(2)}) %all-to-all-start) | async-done | bytes 524320 | tf_op jit(solution)/shard_map/all_to_all | solution.py:103
  78.8 1.9 reduce.5
  80.7 1.3 reshape.252
  85.3 2.3 collective-permute-start
  88.8 3.5 %copy.113 = f32[64,1,2048]{0,1,2:T(1,128)} copy(f32[64,1,2048]{2,1,0:T(1,128)} %param.5) | data formatting | bytes 1048576 | tf_op args[1]
  92.3 11.4 %reduce.6 = f32[2048,64]{1,0:T(8,128)} reduce(f32[2048,1,64]{2,1,0:T(1,128)} %bitcast.104, f32[]{:T(128)} %broadcast.346), dimensions={1}, to_apply=%bitcast.85.reduce_sub_computation | reduce | bytes 1048580
  103.7 2.7 reshape.253
  106.4 4.2 %all-to-all-start.1 = ((f32[16,1,8192]{2,1,0:T(1,128)}), f32[16,1,8192]{2,1,0:T(1,128)}, u32[]{:S(2)}, u32[]{:S(2)}) async-start(f32[16,1,8192]{2,1,0:T(1,128)} %reshape.253), calls=%async_computation.1 | async-start | bytes 1048576 | tf_op jit(solution)/shard_map/all_to_all | solution.py:104
  111.8 3.6 %collective-permute-start.2 = (f32[2,1024,3,1]{1,3,2,0:T(1,128)S(1)}, f32[2,1024,3,1]{1,3,2,0:T(1,128)S(1)}, u32[]{:S(2)}, u32[]{:S(2)}) collective-permute-start(f32[2,1024,3,1]{1,3,2,0:T(1,128)S(1)} %get-tuple-element.8), channel_id=1, source_target_pairs={{0,1},{1,2},{2,3},{3,4},{4,5},{5,6},{6,7},{7,8},{8,9},{9,10},{10,1... | collective-permute-start | bytes 73736 | tf_op jit(solution)/shard_map/ppermute | solution.py:27
  115.5 1.3 collective-permute-start.3
  118.8 5.6 %all-to-all-done.1 = f32[16,1,8192]{2,1,0:T(1,128)} async-done(((f32[16,1,8192]{2,1,0:T(1,128)}), f32[16,1,8192]{2,1,0:T(1,128)}, u32[]{:S(2)}, u32[]{:S(2)}) %all-to-all-start.1) | async-done | bytes 524320 | tf_op jit(solution)/shard_map/all_to_all | solution.py:104
  124.4 3.8 %reduce.7 = f32[16,8192]{1,0:T(8,128)} reduce(f32[16,1,8192]{2,1,0:T(1,128)} %all-to-all-done.1, f32[]{:T(128)} %broadcast.346), dimensions={1}, to_apply=%all_to_all.75.reduce_sub_computation | reduce | bytes 1048580 | tf_op jit(solution)/shard_map/all_to_all | solution.py:104
  128.1 2.4 reshape.254
  130.5 1.7 copy.114
  133.7 4.6 %select_maximum_fusion.5 = f32[2,1026,3,130]{1,3,2,0:T(8,128)S(1)} fusion(f32[2,1024,3,1]{1,3,2,0:T(1,128)S(1)} %collective-permute-done.3, f32[2,1024,3,1]{1,3,2,0:T(1,128)S(1)} %collective-permute-done.2, f32[2,1024,1,128]{1,3,2,0:T(8,128)} %collective-permute-done.1, f32[2,1024,1,128]{1,3,2,0:T(8,128)} %collective-permute-done, ...), kind=kLoop, calls=%fused_computation.26 | loop fusion | flops 11203920 | bytes 6396000 | tf_op jit(solution)/shard_map/concatenate | solution.py:25
  139.6 20.7 %fusion.15 = f32[1024,128]{0,1:T(8,128)S(1)} fusion(s32[1024]{0:T(1024)S(1)} %multiply_add_fusion.4, f32[1024]{0:T(1024)S(1)} %get-tuple-element.29, f32[1024,1,128]{0,2,1:T(8,128)S(1)} %copy.141, f32[1024,1,128]{0,2,1:T(8,128)S(1)} %copy-done.3, f32[1026,3,130]{0,2,1:T(8,128)S(1)} %get-tuple-element.5, f32[1026,3,130]{0,2,1:T(8,128)S(1)} %get-tuple-element.4, ...), kind=kOutput, calls=%fused_computation.35 | convolution fusion | flops 1630928896 | bytes 8396800 | tf_op jit(solution)/shard_map/dot_general | solution.py:77
  160.4 4.6 %collective-permute-start.4 = (f32[1024,1,128]{0,2,1:T(8,128)S(1)}, f32[1024,1,128]{0,2,1:T(8,128)S(1)}, u32[]{:S(2)}, u32[]{:S(2)}) collective-permute-start(f32[1024,1,128]{0,2,1:T(8,128)S(1)} %fusion.119), channel_id=1, source_target_pairs={{0,16},{1,17},{2,18},{3,19},{4,20},{5,21},{6,22},{7,23},{8,24},{9,... | collective-permute-start | bytes 1572872 | tf_op jit(solution)/shard_map/ppermute | solution.py:27
  165.0 1.3 collective-permute-start.5
  166.5 2.3 collective-permute-done.5
  168.8 2.5 collective-permute-start.6
  171.3 1.3 collective-permute-start.7
  172.7 4.2 %collective-permute-done.7 = f32[1024,3,1]{0,2,1:T(1,128)S(1)} collective-permute-done((f32[1024,3,1]{0,2,1:T(1,128)S(1)}, f32[1024,3,1]{0,2,1:T(1,128)S(1)}, u32[]{:S(2)}, u32[]{:S(2)}) %collective-permute-start.7) | collective-permute-done | bytes 12320 | tf_op jit(solution)/shard_map/ppermute | solution.py:29
  177.3 1.3 collective-permute-start.8
  178.7 1.3 collective-permute-start.9
  180.2 2.3 collective-permute-done.9
  183.3 4.6 %collective-permute-start.10 = (f32[1024,3,1]{0,2,1:T(1,128)S(1)}, f32[1024,3,1]{0,2,1:T(1,128)S(1)}, u32[]{:S(2)}, u32[]{:S(2)}) collective-permute-start(f32[1024,3,1]{0,2,1:T(1,128)S(1)} %get-tuple-element.14), channel_id=1, source_target_pairs={{0,1},{1,2},{2,3},{3,4},{4,5},{5,6},{6,7},{7,8},{8,9},{9,10},{10,1... | collective-permute-start | bytes 36872 | tf_op jit(solution)/shard_map/ppermute | solution.py:27
  188.0 1.5 collective-permute-start.11
  190.7 2.9 collective-permute-done.11
  193.5 19.9 %fusion.17 = f32[1024,128]{0,1:T(8,128)S(1)} fusion(f32[1024,128]{0,1:T(8,128)} %copy.142, s32[1024]{0:T(1024)S(1)} %multiply_add_fusion.4, f32[1024]{0:T(1024)S(1)} %get-tuple-element.29, f32[1024,1,128]{0,2,1:T(8,128)S(1)} %fusion.73, f32[1024,3,1]{0,2,1:T(1,128)S(1)} %collective-permute-done.11, f32[1024,1,128]{0,2,1:T(8,128)} %copy-done.1, ...), kind=kOutput, calls=%fused_computation.40 | convolution fusion | flops 1628831744 | bytes 3183104 | tf_op jit(solution)/shard_map/dot_general | solution.py:77
  213.8 1.4 collective-permute-start.12
  215.1 1.3 collective-permute-start.13
  217.3 2.4 collective-permute-done.13
  219.7 4.1 %collective-permute-start.14 = (f32[2,1024,3,1]{1,3,2,0:T(1,128)S(1)}, f32[2,1024,3,1]{1,3,2,0:T(1,128)S(1)}, u32[]{:S(2)}, u32[]{:S(2)}) collective-permute-start(f32[2,1024,3,1]{1,3,2,0:T(1,128)S(1)} %get-tuple-element.6), channel_id=1, source_target_pairs={{0,1},{1,2},{2,3},{3,4},{4,5},{5,6},{6,7},{7,8},{8,9},{9,10},{10,1... | collective-permute-start | bytes 73736 | tf_op jit(solution)/shard_map/ppermute | solution.py:27
  223.8 1.3 collective-permute-start.15
  225.3 4.2 %collective-permute-done.15 = f32[2,1024,3,1]{1,3,2,0:T(1,128)S(1)} collective-permute-done((f32[2,1024,3,1]{1,3,2,0:T(1,128)S(1)}, f32[2,1024,3,1]{1,3,2,0:T(1,128)S(1)}, u32[]{:S(2)}, u32[]{:S(2)}) %collective-permute-start.15) | collective-permute-done | bytes 24608 | tf_op jit(solution)/shard_map/ppermute | solution.py:29
  229.5 3.2 select_maximum_fusion
  233.0 1.7 fusion.43
  234.7 19.3 %fusion.11 = f32[1024,128]{0,1:T(8,128)S(1)} fusion(s32[1024]{0:T(1024)S(1)} %multiply_add_fusion.4, f32[1024]{0:T(1024)S(1)} %get-tuple-element.29, f32[1024,1,128]{0,2,1:T(8,128)S(1)} %fusion.43), kind=kOutput, calls=%fused_computation.33 | convolution fusion | flops 1626341376 | bytes 1056768 | tf_op jit(solution)/shard_map/dot_general | solution.py:77
  254.2 1.3 collective-permute-start.16
  257.0 2.3 collective-permute-done.17
  259.3 4.8 %collective-permute-start.18 = (f32[1024,3,1]{0,2,1:T(1,128)S(1)}, f32[1024,3,1]{0,2,1:T(1,128)S(1)}, u32[]{:S(2)}, u32[]{:S(2)}) collective-permute-start(f32[1024,3,1]{0,2,1:T(1,128)S(1)} %get-tuple-element.12), channel_id=1, source_target_pairs={{0,1},{1,2},{2,3},{3,4},{4,5},{5,6},{6,7},{7,8},{8,9},{9,10},{10,1... | collective-permute-start | bytes 36872 | tf_op jit(solution)/shard_map/ppermute | solution.py:27
  264.2 1.3 collective-permute-start.19
  265.6 4.2 %collective-permute-done.19 = f32[1024,3,1]{0,2,1:T(1,128)S(1)} collective-permute-done((f32[1024,3,1]{0,2,1:T(1,128)S(1)}, f32[1024,3,1]{0,2,1:T(1,128)S(1)}, u32[]{:S(2)}, u32[]{:S(2)}) %collective-permute-start.19) | collective-permute-done | bytes 12320 | tf_op jit(solution)/shard_map/ppermute | solution.py:29
  270.2 1.3 collective-permute-start.20
  273.9 4.4 %all-to-all-start.4 = ((f32[1024,1,128]{2,1,0:T(1,128)}), f32[1024,1,128]{2,1,0:T(1,128)S(1)}, u32[]{:S(2)}, u32[]{:S(2)}) async-start(f32[1024,1,128]{2,1,0:T(1,128)} %copy.149), calls=%async_computation.4 | async-start | bytes 1048576 | tf_op jit(solution)/shard_map/all_to_all | solution.py:121
  278.4 3.8 %collective-permute-start.22 = (f32[1024,3,1]{0,2,1:T(1,128)S(1)}, f32[1024,3,1]{0,2,1:T(1,128)S(1)}, u32[]{:S(2)}, u32[]{:S(2)}) collective-permute-start(f32[1024,3,1]{0,2,1:T(1,128)S(1)} %get-tuple-element.10), channel_id=1, source_target_pairs={{0,1},{1,2},{2,3},{3,4},{4,5},{5,6},{6,7},{7,8},{8,9},{9,10},{10,1... | collective-permute-start | bytes 36872 | tf_op jit(solution)/shard_map/ppermute | solution.py:27
  282.2 1.7 collective-permute-start.23
  283.9 4.0 %collective-permute-done.23 = f32[1024,3,1]{0,2,1:T(1,128)S(1)} collective-permute-done((f32[1024,3,1]{0,2,1:T(1,128)S(1)}, f32[1024,3,1]{0,2,1:T(1,128)S(1)}, u32[]{:S(2)}, u32[]{:S(2)}) %collective-permute-start.23) | collective-permute-done | bytes 12320 | tf_op jit(solution)/shard_map/ppermute | solution.py:29
  287.9 19.3 %fusion.23 = f32[1024,1,128]{0,2,1:T(8,128)} fusion(f32[1024,128]{0,1:T(8,128)S(1)} %fusion.17, s32[1024]{0:T(1024)S(1)} %multiply_add_fusion.4, f32[1024]{0:T(1024)S(1)} %get-tuple-element.29, f32[1024,1,128]{0,2,1:T(8,128)S(1)} %fusion.39, f32[1024,3,1]{0,2,1:T(1,128)S(1)} %collective-permute-done.23, f32[1024,1,128]{0,2,1:T(8,128)S(1)} %collective-permute-done.21, ...), kind=kOutput, calls=%fused_computation.42 | convolution fusion | flops 1628831744 | bytes 3183104 | tf_op jit(solution)/shard_map/dot_general | solution.py:77
  307.2 1.9 copy.147
  309.1 10.4 %all-to-all-start.3 = ((f32[1024,1,128]{2,1,0:T(1,128)}), f32[1024,1,128]{2,1,0:T(1,128)S(1)}, u32[]{:S(2)}, u32[]{:S(2)}) async-start(f32[1024,1,128]{2,1,0:T(1,128)} %copy.147), calls=%async_computation.3 | async-start | bytes 1048576 | tf_op jit(solution)/shard_map/all_to_all | solution.py:120
  320.7 14.2 %all-to-all-done.3 = f32[1024,1,128]{2,1,0:T(1,128)S(1)} async-done(((f32[1024,1,128]{2,1,0:T(1,128)}), f32[1024,1,128]{2,1,0:T(1,128)S(1)}, u32[]{:S(2)}, u32[]{:S(2)}) %all-to-all-start.3) | async-done | bytes 524320 | tf_op jit(solution)/shard_map/all_to_all | solution.py:120
  (65 shorter events, 25.0 us)
Async XLA Ops:
  4.5 29.4 %copy-start = (f32[64,1,2048]{2,1,0:T(1,128)S(1)}, f32[64,1,2048]{2,1,0:T(1,128)}, u32[]{:S(2)}) copy-start(f32[64,1,2048]{2,1,0:T(1,128)} %param.4) | copy-start | bytes 1572868
  25.5 23.5 %all-to-all-start.2 = ((f32[16,1,8192]{2,1,0:T(1,128)}), f32[16,1,8192]{2,1,0:T(1,128)S(1)}, u32[]{:S(2)}, u32[]{:S(2)}) async-start(f32[16,1,8192]{2,1,0:T(1,128)} %reshape.255), calls=%async_computation.2 | async-start | bytes 1048576 | tf_op jit(solution)/shard_map/all_to_all | solution.py:105
  49.0 29.8 %all-to-all-start = ((f32[16,1,8192]{2,1,0:T(1,128)}), f32[16,1,8192]{2,1,0:T(1,128)S(1)}, u32[]{:S(2)}, u32[]{:S(2)}) async-start(f32[16,1,8192]{2,1,0:T(1,128)} %reshape.251), calls=%async_computation | async-start | bytes 1048576 | tf_op jit(solution)/shard_map/all_to_all | solution.py:103
  85.3 25.6 %collective-permute-start = (f32[2,1024,1,128]{1,3,2,0:T(8,128)}, f32[2,1024,1,128]{1,3,2,0:T(8,128)}, u32[]{:S(2)}, u32[]{:S(2)}) collective-permute-start(f32[2,1024,1,128]{1,3,2,0:T(8,128)} %pad_maximum_fusion), channel_id=1, source_target_pairs={{0,16},{1,17},{2,18},{3,19},{4,20},{5,21},{6,22},{7,23},{8,24},{9,... | collective-permute-start | bytes 3145736 | tf_op jit(solution)/shard_map/ppermute | solution.py:27
  87.5 23.3 %collective-permute-start.1 = (f32[2,1024,1,128]{1,3,2,0:T(8,128)}, f32[2,1024,1,128]{1,3,2,0:T(8,128)}, u32[]{:S(2)}, u32[]{:S(2)}) collective-permute-start(f32[2,1024,1,128]{1,3,2,0:T(8,128)} %pad_maximum_fusion), channel_id=1, source_target_pairs={{16,0},{17,1},{18,2},{19,3},{20,4},{21,5},{22,6},{23,7},{24,8},{25... | collective-permute-start | bytes 3145736 | tf_op jit(solution)/shard_map/ppermute | solution.py:29
  106.4 18.0 %all-to-all-start.1 = ((f32[16,1,8192]{2,1,0:T(1,128)}), f32[16,1,8192]{2,1,0:T(1,128)}, u32[]{:S(2)}, u32[]{:S(2)}) async-start(f32[16,1,8192]{2,1,0:T(1,128)} %reshape.253), calls=%async_computation.1 | async-start | bytes 1048576 | tf_op jit(solution)/shard_map/all_to_all | solution.py:104
  111.8 21.8 %collective-permute-start.2 = (f32[2,1024,3,1]{1,3,2,0:T(1,128)S(1)}, f32[2,1024,3,1]{1,3,2,0:T(1,128)S(1)}, u32[]{:S(2)}, u32[]{:S(2)}) collective-permute-start(f32[2,1024,3,1]{1,3,2,0:T(1,128)S(1)} %get-tuple-element.8), channel_id=1, source_target_pairs={{0,1},{1,2},{2,3},{3,4},{4,5},{5,6},{6,7},{7,8},{8,9},{9,10},{10,1... | collective-permute-start | bytes 73736 | tf_op jit(solution)/shard_map/ppermute | solution.py:27
  115.5 18.2 %collective-permute-start.3 = (f32[2,1024,3,1]{1,3,2,0:T(1,128)S(1)}, f32[2,1024,3,1]{1,3,2,0:T(1,128)S(1)}, u32[]{:S(2)}, u32[]{:S(2)}) collective-permute-start(f32[2,1024,3,1]{1,3,2,0:T(1,128)S(1)} %get-tuple-element.9), channel_id=1, source_target_pairs={{1,0},{2,1},{3,2},{4,3},{5,4},{6,5},{7,6},{8,7},{9,8},{10,9},{11,1... | collective-permute-start | bytes 73736 | tf_op jit(solution)/shard_map/ppermute | solution.py:29
  138.4 1.0 copy-start.2
  138.4 1.2 copy-start.3
  160.4 6.0 %collective-permute-start.4 = (f32[1024,1,128]{0,2,1:T(8,128)S(1)}, f32[1024,1,128]{0,2,1:T(8,128)S(1)}, u32[]{:S(2)}, u32[]{:S(2)}) collective-permute-start(f32[1024,1,128]{0,2,1:T(8,128)S(1)} %fusion.119), channel_id=1, source_target_pairs={{0,16},{1,17},{2,18},{3,19},{4,20},{5,21},{6,22},{7,23},{8,24},{9,... | collective-permute-start | bytes 1572872 | tf_op jit(solution)/shard_map/ppermute | solution.py:27
  165.0 3.8 %collective-permute-start.5 = (f32[1024,1,128]{0,2,1:T(8,128)S(1)}, f32[1024,1,128]{0,2,1:T(8,128)S(1)}, u32[]{:S(2)}, u32[]{:S(2)}) collective-permute-start(f32[1024,1,128]{0,2,1:T(8,128)S(1)} %fusion.119), channel_id=1, source_target_pairs={{16,0},{17,1},{18,2},{19,3},{20,4},{21,5},{22,6},{23,7},{24,8},{25... | collective-permute-start | bytes 1572872 | tf_op jit(solution)/shard_map/ppermute | solution.py:29
  168.8 3.9 %collective-permute-start.6 = (f32[1024,3,1]{0,2,1:T(1,128)S(1)}, f32[1024,3,1]{0,2,1:T(1,128)S(1)}, u32[]{:S(2)}, u32[]{:S(2)}) collective-permute-start(f32[1024,3,1]{0,2,1:T(1,128)S(1)} %get-tuple-element.16), channel_id=1, source_target_pairs={{0,1},{1,2},{2,3},{3,4},{4,5},{5,6},{6,7},{7,8},{8,9},{9,10},{10,1... | collective-permute-start | bytes 36872 | tf_op jit(solution)/shard_map/ppermute | solution.py:27
  171.3 5.6 %collective-permute-start.7 = (f32[1024,3,1]{0,2,1:T(1,128)S(1)}, f32[1024,3,1]{0,2,1:T(1,128)S(1)}, u32[]{:S(2)}, u32[]{:S(2)}) collective-permute-start(f32[1024,3,1]{0,2,1:T(1,128)S(1)} %get-tuple-element.17), channel_id=1, source_target_pairs={{1,0},{2,1},{3,2},{4,3},{5,4},{6,5},{7,6},{8,7},{9,8},{10,9},{11,1... | collective-permute-start | bytes 36872 | tf_op jit(solution)/shard_map/ppermute | solution.py:29
  177.3 2.8 collective-permute-start.8
  178.7 3.8 %collective-permute-start.9 = (f32[1024,1,128]{0,2,1:T(8,128)S(1)}, f32[1024,1,128]{0,2,1:T(8,128)S(1)}, u32[]{:S(2)}, u32[]{:S(2)}) collective-permute-start(f32[1024,1,128]{0,2,1:T(8,128)S(1)} %fusion.73), channel_id=1, source_target_pairs={{16,0},{17,1},{18,2},{19,3},{20,4},{21,5},{22,6},{23,7},{24,8},{25... | collective-permute-start | bytes 1572872 | tf_op jit(solution)/shard_map/ppermute | solution.py:29
  182.5 0.8 copy-start.1
  183.3 7.4 %collective-permute-start.10 = (f32[1024,3,1]{0,2,1:T(1,128)S(1)}, f32[1024,3,1]{0,2,1:T(1,128)S(1)}, u32[]{:S(2)}, u32[]{:S(2)}) collective-permute-start(f32[1024,3,1]{0,2,1:T(1,128)S(1)} %get-tuple-element.14), channel_id=1, source_target_pairs={{0,1},{1,2},{2,3},{3,4},{4,5},{5,6},{6,7},{7,8},{8,9},{9,10},{10,1... | collective-permute-start | bytes 36872 | tf_op jit(solution)/shard_map/ppermute | solution.py:27
  188.0 5.6 %collective-permute-start.11 = (f32[1024,3,1]{0,2,1:T(1,128)S(1)}, f32[1024,3,1]{0,2,1:T(1,128)S(1)}, u32[]{:S(2)}, u32[]{:S(2)}) collective-permute-start(f32[1024,3,1]{0,2,1:T(1,128)S(1)} %get-tuple-element.15), channel_id=1, source_target_pairs={{1,0},{2,1},{3,2},{4,3},{5,4},{6,5},{7,6},{8,7},{9,8},{10,9},{11,1... | collective-permute-start | bytes 36872 | tf_op jit(solution)/shard_map/ppermute | solution.py:29
  213.8 3.6 %collective-permute-start.12 = (f32[2,1024,1,128]{1,3,2,0:T(8,128)S(1)}, f32[2,1024,1,128]{1,3,2,0:T(8,128)S(1)}, u32[]{:S(2)}, u32[]{:S(2)}) collective-permute-start(f32[2,1024,1,128]{1,3,2,0:T(8,128)S(1)} %pad_maximum_fusion.1), channel_id=1, source_target_pairs={{0,16},{1,17},{2,18},{3,19},{4,20},{5,21},{6,22},{7,23},{8,24},{9,... | collective-permute-start | bytes 3145736 | tf_op jit(solution)/shard_map/ppermute | solution.py:27
  215.1 4.6 %collective-permute-start.13 = (f32[2,1024,1,128]{1,3,2,0:T(8,128)S(1)}, f32[2,1024,1,128]{1,3,2,0:T(8,128)S(1)}, u32[]{:S(2)}, u32[]{:S(2)}) collective-permute-start(f32[2,1024,1,128]{1,3,2,0:T(8,128)S(1)} %pad_maximum_fusion.1), channel_id=1, source_target_pairs={{16,0},{17,1},{18,2},{19,3},{20,4},{21,5},{22,6},{23,7},{24,8},{25... | collective-permute-start | bytes 3145736 | tf_op jit(solution)/shard_map/ppermute | solution.py:29
  219.7 5.6 %collective-permute-start.14 = (f32[2,1024,3,1]{1,3,2,0:T(1,128)S(1)}, f32[2,1024,3,1]{1,3,2,0:T(1,128)S(1)}, u32[]{:S(2)}, u32[]{:S(2)}) collective-permute-start(f32[2,1024,3,1]{1,3,2,0:T(1,128)S(1)} %get-tuple-element.6), channel_id=1, source_target_pairs={{0,1},{1,2},{2,3},{3,4},{4,5},{5,6},{6,7},{7,8},{8,9},{9,10},{10,1... | collective-permute-start | bytes 73736 | tf_op jit(solution)/shard_map/ppermute | solution.py:27
  223.8 5.7 %collective-permute-start.15 = (f32[2,1024,3,1]{1,3,2,0:T(1,128)S(1)}, f32[2,1024,3,1]{1,3,2,0:T(1,128)S(1)}, u32[]{:S(2)}, u32[]{:S(2)}) collective-permute-start(f32[2,1024,3,1]{1,3,2,0:T(1,128)S(1)} %get-tuple-element.7), channel_id=1, source_target_pairs={{1,0},{2,1},{3,2},{4,3},{5,4},{6,5},{7,6},{8,7},{9,8},{10,9},{11,1... | collective-permute-start | bytes 73736 | tf_op jit(solution)/shard_map/ppermute | solution.py:29
  254.2 2.8 collective-permute-start.16
  255.5 3.8 %collective-permute-start.17 = (f32[1024,1,128]{0,2,1:T(8,128)S(1)}, f32[1024,1,128]{0,2,1:T(8,128)S(1)}, u32[]{:S(2)}, u32[]{:S(2)}) collective-permute-start(f32[1024,1,128]{0,2,1:T(8,128)S(1)} %fusion.120), channel_id=1, source_target_pairs={{16,0},{17,1},{18,2},{19,3},{20,4},{21,5},{22,6},{23,7},{24,8},{25... | collective-permute-start | bytes 1572872 | tf_op jit(solution)/shard_map/ppermute | solution.py:29
  259.3 6.2 %collective-permute-start.18 = (f32[1024,3,1]{0,2,1:T(1,128)S(1)}, f32[1024,3,1]{0,2,1:T(1,128)S(1)}, u32[]{:S(2)}, u32[]{:S(2)}) collective-permute-start(f32[1024,3,1]{0,2,1:T(1,128)S(1)} %get-tuple-element.12), channel_id=1, source_target_pairs={{0,1},{1,2},{2,3},{3,4},{4,5},{5,6},{6,7},{7,8},{8,9},{9,10},{10,1... | collective-permute-start | bytes 36872 | tf_op jit(solution)/shard_map/ppermute | solution.py:27
  264.2 5.6 %collective-permute-start.19 = (f32[1024,3,1]{0,2,1:T(1,128)S(1)}, f32[1024,3,1]{0,2,1:T(1,128)S(1)}, u32[]{:S(2)}, u32[]{:S(2)}) collective-permute-start(f32[1024,3,1]{0,2,1:T(1,128)S(1)} %get-tuple-element.13), channel_id=1, source_target_pairs={{1,0},{2,1},{3,2},{4,3},{5,4},{6,5},{7,6},{8,7},{9,8},{10,9},{11,1... | collective-permute-start | bytes 36872 | tf_op jit(solution)/shard_map/ppermute | solution.py:29
  270.2 8.1 %collective-permute-start.20 = (f32[1024,1,128]{0,2,1:T(8,128)S(1)}, f32[1024,1,128]{0,2,1:T(8,128)S(1)}, u32[]{:S(2)}, u32[]{:S(2)}) collective-permute-start(f32[1024,1,128]{0,2,1:T(8,128)S(1)} %fusion.39), channel_id=1, source_target_pairs={{0,16},{1,17},{2,18},{3,19},{4,20},{5,21},{6,22},{7,23},{8,24},{9,... | collective-permute-start | bytes 1572872 | tf_op jit(solution)/shard_map/ppermute | solution.py:27
  271.6 6.8 %collective-permute-start.21 = (f32[1024,1,128]{0,2,1:T(8,128)S(1)}, f32[1024,1,128]{0,2,1:T(8,128)S(1)}, u32[]{:S(2)}, u32[]{:S(2)}) collective-permute-start(f32[1024,1,128]{0,2,1:T(8,128)S(1)} %fusion.39), channel_id=1, source_target_pairs={{16,0},{17,1},{18,2},{19,3},{20,4},{21,5},{22,6},{23,7},{24,8},{25... | collective-permute-start | bytes 1572872 | tf_op jit(solution)/shard_map/ppermute | solution.py:29
  273.9 35.2 %all-to-all-start.4 = ((f32[1024,1,128]{2,1,0:T(1,128)}), f32[1024,1,128]{2,1,0:T(1,128)S(1)}, u32[]{:S(2)}, u32[]{:S(2)}) async-start(f32[1024,1,128]{2,1,0:T(1,128)} %copy.149), calls=%async_computation.4 | async-start | bytes 1048576 | tf_op jit(solution)/shard_map/all_to_all | solution.py:121
  278.4 5.5 %collective-permute-start.22 = (f32[1024,3,1]{0,2,1:T(1,128)S(1)}, f32[1024,3,1]{0,2,1:T(1,128)S(1)}, u32[]{:S(2)}, u32[]{:S(2)}) collective-permute-start(f32[1024,3,1]{0,2,1:T(1,128)S(1)} %get-tuple-element.10), channel_id=1, source_target_pairs={{0,1},{1,2},{2,3},{3,4},{4,5},{5,6},{6,7},{7,8},{8,9},{9,10},{10,1... | collective-permute-start | bytes 36872 | tf_op jit(solution)/shard_map/ppermute | solution.py:27
  282.2 5.7 %collective-permute-start.23 = (f32[1024,3,1]{0,2,1:T(1,128)S(1)}, f32[1024,3,1]{0,2,1:T(1,128)S(1)}, u32[]{:S(2)}, u32[]{:S(2)}) collective-permute-start(f32[1024,3,1]{0,2,1:T(1,128)S(1)} %get-tuple-element.11), channel_id=1, source_target_pairs={{1,0},{2,1},{3,2},{4,3},{5,4},{6,5},{7,6},{8,7},{9,8},{10,9},{11,1... | collective-permute-start | bytes 36872 | tf_op jit(solution)/shard_map/ppermute | solution.py:29
  309.1 25.7 %all-to-all-start.3 = ((f32[1024,1,128]{2,1,0:T(1,128)}), f32[1024,1,128]{2,1,0:T(1,128)S(1)}, u32[]{:S(2)}, u32[]{:S(2)}) async-start(f32[1024,1,128]{2,1,0:T(1,128)} %copy.147), calls=%async_computation.3 | async-start | bytes 1048576 | tf_op jit(solution)/shard_map/all_to_all | solution.py:120
where the time goes:
time: 340 us; the launch traced here: 336 us
  starting transfers between devices  94.4 us (28%)
  matrix products  79.2 us (23%)
  waiting for transfers between devices  63.3 us (19%)
  other arithmetic  62 us (18%)
  local copies, waits for them, and re-layouts  35.8 us (11%)
    dot_general x4, matrix products, apply_table(): jnp.dot(matrix, flat, precision=lax.Precision.HIGHEST, preferred_element_...  79.2 us
    unnamed x4, other arithmetic  39.8 us
    ppermute x12, starting transfers between devices, extended(): lax.ppermute(tail, axis, [(i, (i + 1) % count) for i in range(ends)])  35.6 us
    ppermute x12, waiting for transfers between devices, extended(): lax.ppermute(head, axis, [((i + 1) % count, i) for i in range(ends)])  28.8 us
    unnamed x18, local copies, waits for them, and re-layouts  19.3 us
    ppermute x12, starting transfers between devices, extended(): lax.ppermute(head, axis, [((i + 1) % count, i) for i in range(ends)])  16.1 us
    all_to_all x1, starting transfers between devices, per_device(): lax.all_to_all(pressure, 'strike', split_axis=2, concat_axis=0, tiled=True)  15.4 us
    all_to_all x1, waiting for transfers between devices, per_device(): lax.all_to_all(field, 'strike', split_axis=0, concat_axis=2, tiled=True)  14.2 us
  transfers between devices with their start and end apart: 29, of which 20 were waited for; matrix products, arithmetic and copies ran while one was open for 21% of the time, Pallas kernels for 0%

commit v1 on v0

v1 whole, which is shorter than its diff:
```python
import functools
import math

import jax
import jax.numpy as jnp
from jax import lax
from jax.experimental import pallas as pl
from jax.experimental.pallas import tpu as pltpu
from jax.sharding import PartitionSpec as P

CLASSES = 8
DEFECT = 2
SWEEPS = 3

STORE = 0.5
LOW = 0.05
HIGH = 1.95

SUB = 8
LANES = 128
HALF = LANES // 2
MESH = pl.DeviceIdType.MESH


def chebyshev_weights(count):
    middle = 0.5 * (LOW + HIGH)
    half = 0.5 * (HIGH - LOW)
    return [
        1.0 / (middle + half * math.cos(math.pi * (2 * j + 1) / (2 * count))) for j in range(count)
    ]


def lookup(classes, table):
    base = jnp.zeros(classes.shape, jnp.float32)
    for code in range(CLASSES):
        base = jnp.where(classes == code, table[code], base)
    return base


def power(x, count):
    result = None
    while count:
        if count & 1:
            result = x if result is None else result * x
        count >>= 1
        if count:
            x = x * x
    return result


def group_size(count):
    low = 1
    while low * low < count:
        low *= 2
    return low if count % low == 0 else count


def kernel(
    crosses, strikes, dips, xin, out, x, rims, mob, res, ans, part, qpow, col, rim_ans, rim_base,
    near_box, far_box, cross_sems, own_sem, rim_sems, near_sems, far_sems, out_sems, out_own,
):
    tiles, width = x.shape[2], x.shape[4]
    main = width - LANES
    rows = tiles * SUB
    members = near_box.shape[1]
    groups = far_box.shape[1]
    cross = lax.axis_index("cross")
    strike = lax.axis_index("strike")
    member = lax.rem(strike, members)
    group = lax.div(strike, members)

    def across(k):
        return lax.rem(cross + k, crosses)

    def before(k):
        return lax.rem(cross + crosses - k, crosses)

    up = lax.rem(strike + 1, strikes)
    down = lax.rem(strike + strikes - 1, strikes)

    def near_peer(k):
        return (cross, group * members + lax.rem(member + k, members))

    def far_peer(k):
        return (cross, lax.rem(group + k, groups) * members + member)

    barrier = pltpu.get_barrier_semaphore()
    peers = [(across(k), strike) for k in range(1, crosses)]
    peers += [(across(k), side) for k in range(crosses) for side in (up, down)]
    peers += [near_peer(k) for k in range(1, members)]
    peers += [far_peer(k) for k in range(1, groups)]
    for peer in peers:
        pl.semaphore_signal(barrier, inc=1, device_id=peer, device_id_type=MESH)
    pl.semaphore_wait(barrier, len(peers))

    own = pltpu.make_async_copy(xin.at[cross], x.at[cross], own_sem)
    own.start()
    rim_copies = []
    for k in range(crosses):
        for side, target, tile, row in ((0, up, tiles - 1, SUB - 1), (1, down, 0, 0)):
            rim_copies.append(
                pltpu.make_async_remote_copy(
                    src_ref=xin.at[across(k), pl.ds(0, 2), tile, pl.ds(row, 1), :],
                    dst_ref=rims.at[side, cross],
                    send_sem=rim_sems.at[0, side, k],
                    recv_sem=rim_sems.at[1, side, k],
                    device_id=(across(k), target),
                    device_id_type=MESH,
                )
            )
    cross_copies = [
        pltpu.make_async_remote_copy(
            src_ref=xin.at[across(k)],
            dst_ref=x.at[cross],
            send_sem=cross_sems.at[0, k - 1],
            recv_sem=cross_sems.at[1, k - 1],
            device_id=(across(k), strike),
            device_id_type=MESH,
        )
        for k in range(1, crosses)
    ]
    for copy in cross_copies + rim_copies:
        copy.start()
    own.wait()
    for k in range(1, crosses):
        pltpu.make_async_remote_copy(
            src_ref=x.at[before(k)],
            dst_ref=x.at[before(k)],
            send_sem=cross_sems.at[0, k - 1],
            recv_sem=cross_sems.at[1, k - 1],
            device_id=(across(k), strike),
            device_id_type=MESH,
        ).wait_recv()
    for k in range(crosses):
        for side, target in ((0, up), (1, down)):
            pltpu.make_async_remote_copy(
                src_ref=rims.at[side, before(k)],
                dst_ref=rims.at[side, before(k)],
                send_sem=rim_sems.at[0, side, k],
                recv_sem=rim_sems.at[1, side, k],
                device_id=(across(k), target),
                device_id_type=MESH,
            ).wait_recv()
    for copy in cross_copies + rim_copies:
        copy.wait_send()

    inside = (strike > 0, strike < strikes - 1)
    lane = lax.broadcasted_iota(jnp.int32, (1, 1, width), 2)
    valid = (
        (lane < main)
        | ((lane < main + HALF) & (cross < crosses - 1))
        | ((lane >= main + HALF) & (cross > 0))
    )
    sub = lax.broadcasted_iota(jnp.int32, (crosses, SUB, width), 1)
    none = jnp.zeros((1, SUB, width), jnp.float32)

    for side in range(2):
        rim_ans[side, 1] = jnp.where(inside[side], rims[side, :, 0], 0.0)
        rim_base[side] = jnp.where(inside[side], rims[side, :, 1], 0.0)

    def left(a):
        return pltpu.roll(a, 1, 2)

    def right(a):
        return pltpu.roll(a, width - 1, 2)

    def later(a, k):
        return pltpu.roll(a, k, 1)

    def sooner(a, k):
        return pltpu.roll(a, SUB - k, 1)

    def mobility(base, p):
        return base * (1.0 + 0.5 * jnp.tanh(p))

    def trade(box, sems, slot, count, peer_of, mine, parity):
        box[parity, mine] = slot
        copies = []
        for k in range(1, count):
            copy = pltpu.make_async_remote_copy(
                src_ref=box.at[parity, mine],
                dst_ref=box.at[parity, mine],
                send_sem=sems.at[0, parity, k - 1],
                recv_sem=sems.at[1, parity, k - 1],
                device_id=peer_of(k),
                device_id_type=MESH,
            )
            copy.start()
            copies.append(copy)

        def finish():
            for k in range(1, count):
                origin = lax.rem(mine + count - k, count)
                pltpu.make_async_remote_copy(
                    src_ref=box.at[parity, origin],
                    dst_ref=box.at[parity, origin],
                    send_sem=sems.at[0, parity, k - 1],
                    recv_sem=sems.at[1, parity, k - 1],
                    device_id=peer_of(k),
                    device_id_type=MESH,
                ).wait_recv()
            for copy in copies:
                copy.wait_send()

        return finish

    def trade_near(slot, parity):
        return trade(near_box, near_sems, slot, members, near_peer, member, parity)

    def trade_far(slot, parity):
        return trade(far_box, far_sems, slot, groups, far_peer, group, parity)

    omega = chebyshev_weights(SWEEPS)

    def one_step(step, carry):
        turn = step * (SWEEPS + 1)
        parity = lax.rem(turn, 2)
        total = jnp.zeros((crosses, SUB, width), jnp.float32)
        for t in range(tiles):
            m = mobility(x[:, 1, t], x[:, 0, t])
            mob[t] = m
            total = total + m
        total = jnp.sum(total, axis=1, keepdims=True)
        finish = trade_near(jnp.stack([total, total]), parity)

        rim_p = [rim_ans[side, 1] for side in range(2)]
        rim_m = [mobility(rim_base[side], rim_p[side]) for side in range(2)]
        first_p, first_m = x[:, 0, 0], mob[0]
        last_p, last_m = x[:, 0, tiles - 1], mob[tiles - 1]
        p_was = jnp.where(sub == 0, rim_p[0], later(last_p, 1))
        m_was = jnp.where(sub == 0, rim_m[0], later(last_m, 1))
        p, m = first_p, first_m
        flux = 0.5 * (m + m_was) * (p - p_was)
        for t in range(tiles):
            if t + 1 < tiles:
                p_next, m_next = x[:, 0, t + 1], mob[t + 1]
            else:
                p_next = jnp.where(sub == SUB - 1, rim_p[1], sooner(first_p, 1))
                m_next = jnp.where(sub == SUB - 1, rim_m[1], sooner(first_m, 1))
            flux_next = 0.5 * (m_next + m) * (p_next - p)
            along = 0.5 * (m + left(m)) * (p - left(p))
            p_wide = jnp.concatenate([none, p, none], axis=0)
            m_wide = jnp.concatenate([none, m, none], axis=0)
            over = 0.5 * (m_wide[1:] + m_wide[:-1]) * (p_wide[1:] - p_wide[:-1])
            applied = STORE * p + (flux - flux_next) + (along - right(along)) + (over[:-1] - over[1:])
            res[:, t] = jnp.where(valid, x[:, 2, t] - applied, 0.0)
            ans[t] = jnp.zeros_like(p)
            p, m, flux = p_next, m_next, flux_next

        finish()
        total = near_box[parity, 0, 0]
        for a in range(1, members):
            total = total + near_box[parity, a, 0]
        trade_far(jnp.stack([total, total]), parity)()
        total = far_box[parity, 0, 0]
        for a in range(1, groups):
            total = total + far_box[parity, a, 0]
        mref = total * (1.0 / dips)

        root = jnp.sqrt((STORE + 4.0 * mref) * (STORE + 8.0 * mref))
        q = 2.0 * mref / (STORE + 6.0 * mref + root)
        gain = 1.0 / root
        chunk = power(q, tiles)
        block = power(q, rows)
        cluster = power(block, members)
        whole = power(cluster, groups)
        unmirror = 1.0 / (1.0 - whole * whole)
        col[0], col[1], col[2], col[3], col[4], col[5], col[6], col[7] = (
            mref, q, gain, chunk, block, cluster, whole, unmirror
        )
        running = q
        for t in range(tiles):
            qpow[t] = running
            running = running * q
        ahead = jnp.ones((crosses, SUB, width), jnp.float32)
        behind = ahead
        step_up = jnp.broadcast_to(chunk, ahead.shape)
        for bit in (1, 2, 4):
            ahead = jnp.where((sub & bit) != 0, ahead * step_up, ahead)
            behind = jnp.where((sub & bit) == 0, behind * step_up, behind)
            step_up = step_up * step_up
        part[0], part[1] = ahead, behind
        for side in range(2):
            rim_ans[side, 0] = jnp.zeros((crosses, 1, width), jnp.float32)

        def sweep(j, carry):
            parity = lax.rem(turn + 1 + j, 2)
            weight = jnp.float32(omega[0])
            for i in range(1, SWEEPS):
                weight = jnp.where(j == i, jnp.float32(omega[i]), weight)
            keep = 1.0 - weight
            mref, q, chunk = col[0], col[1], col[3]

            y = jnp.zeros((crosses, SUB, width), jnp.float32)
            for t in range(tiles):
                u = ans[t]
                near = left(u) + right(u)
                if crosses > 1:
                    near = near + jnp.concatenate([none, u[:-1]], axis=0)
                    near = near + jnp.concatenate([u[1:], none], axis=0)
                r = res[:, t] + mref * near
                mob[t] = r
                y = r + q * y
                qv = y - r
                part[2 + t] = qv
            z = jnp.zeros((crosses, SUB, width), jnp.float32)
            for t in reversed(range(tiles)):
                z = mob[t] + q * z
                part[2 + t] = part[2 + t] + z
            step_up = chunk
            for k in (1, 2, 4):
                y = y + step_up * jnp.where(sub >= k, later(y, k), 0.0)
                z = z + step_up * jnp.where(sub < SUB - k, sooner(z, k), 0.0)
                step_up = step_up * step_up
            tail, head = y[:, SUB - 1 :, :], z[:, :1, :]
            trade_near(jnp.stack([tail, head]), parity)()

            block, cluster, whole, unmirror = col[4], col[5], col[6], col[7]
            fore = near_box[parity, 0, 0]
            back = near_box[parity, members - 1, 1]
            for a in range(1, members):
                fore = fore * block + near_box[parity, a, 0]
                back = back * block + near_box[parity, members - 1 - a, 1]
            trade_far(jnp.stack([fore, back]), parity)()
            fore = far_box[parity, 0, 0]
            back = far_box[parity, groups - 1, 1]
            for a in range(1, groups):
                fore = fore * cluster + far_box[parity, a, 0]
                back = back * cluster + far_box[parity, groups - 1 - a, 1]
            from_left = (back + whole * fore) * unmirror
            from_right = (fore + whole * back) * unmirror
            for a in range(groups - 1):
                b = groups - 1 - a
                from_left = jnp.where(
                    a < group, from_left * cluster + far_box[parity, a, 0], from_left
                )
                from_right = jnp.where(
                    b > group, from_right * cluster + far_box[parity, b, 1], from_right
                )
            for a in range(members - 1):
                b = members - 1 - a
                from_left = jnp.where(
                    a < member, from_left * block + near_box[parity, a, 0], from_left
                )
                from_right = jnp.where(
                    b > member, from_right * block + near_box[parity, b, 1], from_right
                )

            scale = weight * col[2]
            rim_ans[0, 0] = keep * rim_ans[0, 0] + scale * (
                from_left + q * (head + block * from_right)
            )
            rim_ans[1, 0] = keep * rim_ans[1, 0] + scale * (
                from_right + q * (tail + block * from_left)
            )
            y = jnp.where(sub >= 1, later(y, 1), 0.0) + part[0] * from_left
            z = jnp.where(sub < SUB - 1, sooner(z, 1), 0.0) + part[1] * from_right
            for t in range(tiles):
                solved = part[2 + t] + qpow[t] * y + qpow[tiles - 1 - t] * z
                ans[t] = keep * ans[t] + scale * solved
            return carry

        lax.fori_loop(0, SWEEPS, sweep, 0)
        for t in range(tiles):
            x[:, 0, t] = x[:, 0, t] + ans[t]
        for side in range(2):
            rim_ans[side, 1] = rim_ans[side, 1] + jnp.where(inside[side], rim_ans[side, 0], 0.0)
        return carry

    lax.fori_loop(0, DEFECT, one_step, 0)

    keeps = [
        pltpu.make_async_copy(x.at[cross, 0, :, :, pl.ds(0, main)], out.at[0, cross], out_own.at[0]),
        pltpu.make_async_copy(res.at[cross, :, :, pl.ds(0, main)], out.at[1, cross], out_own.at[1]),
    ]
    gives = []
    for k in range(1, crosses):
        for which in range(2):
            source = x.at[across(k), 0] if which == 0 else res.at[across(k)]
            gives.append(
                pltpu.make_async_remote_copy(
                    src_ref=source.at[:, :, pl.ds(0, main)],
                    dst_ref=out.at[which, cross],
                    send_sem=out_sems.at[0, which, k - 1],
                    recv_sem=out_sems.at[1, which, k - 1],
                    device_id=(across(k), strike),
                    device_id_type=MESH,
                )
            )
    for copy in gives + keeps:
        copy.start()
    for copy in keeps:
        copy.wait()
    for k in range(1, crosses):
        for which in range(2):
            pltpu.make_async_remote_copy(
                src_ref=out.at[which, before(k)],
                dst_ref=out.at[which, before(k)],
                send_sem=out_sems.at[0, which, k - 1],
                recv_sem=out_sems.at[1, which, k - 1],
                device_id=(across(k), strike),
                device_id_type=MESH,
            ).wait_recv()
    for copy in gives:
        copy.wait_send()


def per_device(pressure, source, facies, mobility_table):
    crosses = lax.axis_size("cross")
    strikes = lax.axis_size("strike")
    rows, _, cells = pressure.shape
    tiles = rows // SUB
    main = cells // crosses
    width = main + LANES
    members = group_size(strikes)
    groups = strikes // members

    base = lookup(facies, mobility_table)

    def dealt(a):
        return a.reshape(SUB, tiles, cells).transpose(1, 0, 2)

    whole = jnp.stack([dealt(pressure), dealt(base), dealt(source)])
    empty = jnp.zeros(whole.shape[:-1] + (LANES,), jnp.float32)
    low = lax.broadcasted_iota(jnp.int32, empty.shape, 3) < HALF
    windows = []
    for k in range(crosses):
        after = whole[..., (k + 1) * main : (k + 1) * main + LANES] if k + 1 < crosses else empty
        ahead = whole[..., k * main - LANES : k * main] if k > 0 else empty
        windows.append(
            jnp.concatenate(
                [whole[..., k * main : (k + 1) * main], jnp.where(low, after, ahead)], axis=-1
            )
        )
    xin = jnp.stack(windows)

    f32 = jnp.float32
    vm = pltpu.VMEM
    dma = pltpu.SemaphoreType.DMA
    field = (tiles, crosses, SUB, width)
    thin = (crosses, 1, width)
    out = pl.pallas_call(
        functools.partial(kernel, crosses, strikes, rows * strikes),
        out_shape=jax.ShapeDtypeStruct((2, crosses, tiles, SUB, main), f32),
        in_specs=[pl.BlockSpec(memory_space=pl.ANY)],
        out_specs=pl.BlockSpec(memory_space=pl.ANY),
        scratch_shapes=[
            vm((crosses, 3, tiles, SUB, width), f32),
            vm((2, crosses, 2, 1, width), f32),
            vm(field, f32),
            vm((crosses, tiles, SUB, width), f32),
            vm(field, f32),
            vm((tiles + 2,) + field[1:], f32),
            vm((tiles,) + thin, f32),
            vm((8,) + thin, f32),
            vm((2, 2) + thin, f32),
            vm((2,) + thin, f32),
            vm((2, members, 2) + thin, f32),
            vm((2, groups, 2) + thin, f32),
            dma((2, max(crosses - 1, 1))),
            dma,
            dma((2, 2, crosses)),
            dma((2, 2, max(members - 1, 1))),
            dma((2, 2, max(groups - 1, 1))),
            dma((2, 2, max(crosses - 1, 1))),
            dma((2,)),
        ],
        compiler_params=pltpu.CompilerParams(
            collective_id=0, has_side_effects=True, vmem_limit_bytes=40 * 1024 * 1024
        ),
    )(xin)

    def gathered(a):
        return a.transpose(2, 1, 0, 3).reshape(rows, 1, cells)

    return gathered(out[0]), gathered(out[1])


def solution(mesh):
    in_specs = (
        P("strike", "cross", None),
        P("strike", "cross", None),
        P("strike", "cross", None),
        P(),
    )
    out_specs = (P("strike", "cross", None), P("strike", "cross", None))
    return jax.shard_map(
        per_device, mesh=mesh, in_specs=in_specs, out_specs=out_specs, check_vma=False
    )
```

time: 340 us -> 90.5 us (0.27); the launches traced: 336 us -> 90.2 us
  starting transfers between devices: 94.4 us -> 0 us
  matrix products: 79.2 us -> 0 us
  Pallas kernels: 0 us -> 75.2 us
  waiting for transfers between devices: 63.3 us -> 0 us
  other arithmetic: 62 us -> 6.9 us
  local copies, waits for them, and re-layouts: 35.8 us -> 7.33 us
    dot_general x4 -> x0, matrix products: 79.2 us -> none  [apply_table(): jnp.dot(matrix, flat, precision=lax.Precision.HIGHEST, preferred_element_...]
    pallas_call x0 -> x1, Pallas kernels: none -> 75.2 us  [per_device(): pl.pallas_call(functools.partial(kernel, crosses, strikes, rows * strikes...]
    ppermute x24 -> x0, starting transfers between devices: 51.7 us -> none  [the longest x12 35.6 us: extended(): lax.ppermute(tail, axis, [(i, (i + 1) % count) for i in range(ends)])]
    all_to_all x5 -> x0, starting transfers between devices: 42.7 us -> none  [the longest x1 15.4 us: per_device(): lax.all_to_all(pressure, 'strike', split_axis=2, concat_axis=0, tiled=True)]
    unnamed x4 -> x0, other arithmetic: 39.8 us -> none
    all_to_all x5 -> x0, waiting for transfers between devices: 32.6 us -> none  [the longest x1 14.2 us: per_device(): lax.all_to_all(field, 'strike', split_axis=0, concat_axis=2, tiled=True)]
    ppermute x24 -> x0, waiting for transfers between devices: 30.6 us -> none  [the longest x12 28.8 us: extended(): lax.ppermute(head, axis, [((i + 1) % count, i) for i in range(ends)])]
    unnamed x18 -> x6, local copies, waits for them, and re-layouts: 19.3 us -> 0.56 us
  transfers between devices with their start and end apart: 29 -> 0, of which waited for: 20 -> 0; matrix products, arithmetic and copies ran while one was open for 21% -> 0% of each run, Pallas kernels for 0% -> 0%
where the time goes in v1:
time: 90.5 us; the launch traced here: 90.2 us
  Pallas kernels  75.2 us (83%)
  local copies, waits for them, and re-layouts  7.33 us (8%)
  other arithmetic  6.9 us (8%)
    pallas_call x1, Pallas kernels, per_device(): pl.pallas_call(functools.partial(kernel, crosses, strikes, rows * strikes...  75.2 us
    reshape x1, other arithmetic, dealt(): return a.reshape(SUB, tiles, cells).transpose(1, 0, 2)  6.47 us
    reshape x2, local copies, waits for them, and re-layouts, gathered(): return a.transpose(2, 1, 0, 3).reshape(rows, 1, cells)  3.21 us

profile of v1, /device:TPU:0, one launch (start us, length us, event | category | flops | bytes accessed | tf_op | source)
XLA Modules:
  0.0 90.2 jit_solution(7818010264239642569)
XLA Ops:
  0.6 0.0 copy-start
  0.7 1.6 %fusion.1 = (f32[1]{0:T(128)}, f32[1]{0:T(128)}, f32[1]{0:T(128)}, f32[1]{0:T(128)}, f32[1]{0:T(128)}, /*index=5*/f32[1]{0:T(128)}, f32[1]{0:T(128)}, f32[1]{0:T(128)}) fusion(f32[8]{0:T(128)} %param.7), kind=kLoop, calls=%fused_computation.16 | loop fusion | bytes 64 | tf_op jit(solution)/shard_map/slice | solution.py:36
  2.3 6.5 %select_bitcast_fusion = f32[8,8,2048]{2,1,0:T(8,128)S(1)} fusion(s32[64,1,2048]{2,1,0:T(1,128)} %param.6, f32[]{:T(128)} %bitcast.9, f32[]{:T(128)} %bitcast.8, f32[]{:T(128)} %bitcast.7, f32[]{:T(128)} %bitcast.6, f32[]{:T(128)} %bitcast.5, f32[]{:T(128)} %bitcast.4, f32[]{:T(128)} %bitcast.3, f32[]{:T(128)} %bitcast.2), kind=kLoop, calls=%fused_computation.11 | loop fusion | flops 2097152 | bytes 1048608 | tf_op jit(solution)/shard_map/reshape | solution.py:421
  8.8 0.0 copy-start.1
  8.8 0.3 copy.32
  9.1 0.0 copy-done
  9.1 0.2 copy.30
  9.3 0.3 copy.33
  9.6 0.2 copy-done.1
  9.8 0.2 copy.29
  10.0 0.3 copy.31
  10.3 0.1 pad_maximum_fusion.1
  10.5 0.1 fusion
  10.6 0.1 maximum_bitcast_fusion
  10.7 0.1 pad_maximum_fusion.xin
  10.8 75.2 %shard_map.59 = f32[2,2,8,8,1024]{4,3,2,1,0:T(8,128)S(1)} custom-call(f32[2,3,8,8,1152]{4,3,2,1,0:T(8,128)S(1)} %pad_maximum_fusion.xin), custom_call_target="tpu_custom_call" | custom-call | tf_op jit(solution)/shard_map/pallas_call | solution.py:442
  86.1 0.1 slice_bitcast_fusion
  86.2 0.4 copy.18
  86.6 1.6 %reshape.25 = f32[64,1,2048]{2,1,0:T(1,128)} reshape(f32[8,8,2,1024]{3,2,1,0:T(2,128)S(1)} %copy.18) | data formatting | bytes 1048576 | tf_op jit(solution)/shard_map/reshape | solution.py:474
  88.2 0.4 copy.17
  88.6 1.6 %reshape.24 = f32[64,1,2048]{2,1,0:T(1,128)} reshape(f32[8,8,2,1024]{3,2,1,0:T(2,128)S(1)} %copy.17) | data formatting | bytes 1048576 | tf_op jit(solution)/shard_map/reshape | solution.py:474
  (2 shorter events, 0.0 us)
Async XLA Ops:
  0.6 8.5 %copy-start = (f32[64,1,2048]{2,1,0:T(1,128)S(1)}, f32[64,1,2048]{2,1,0:T(1,128)}, u32[]{:S(2)}) copy-start(f32[64,1,2048]{2,1,0:T(1,128)} %param.4) | copy-start | bytes 1572868
  8.8 1.0 %copy-start.1 = (f32[64,1,2048]{2,1,0:T(1,128)S(1)}, f32[64,1,2048]{2,1,0:T(1,128)}, u32[]{:S(2)}) copy-start(f32[64,1,2048]{2,1,0:T(1,128)} %param.5) | copy-start | bytes 1572868

commit v2 on v1

v2 whole, which is shorter than its diff:
```python
import functools
import math

import jax
import jax.numpy as jnp
from jax import lax
from jax.experimental import pallas as pl
from jax.experimental.pallas import tpu as pltpu
from jax.sharding import PartitionSpec as P

CLASSES = 8
DEFECT = 2
SWEEPS = 3

STORE = 0.5
LOW = 0.05
HIGH = 1.95

SUB = 8
LANES = 128
HALF = LANES // 2
MESH = pl.DeviceIdType.MESH


def chebyshev_weights(count):
    middle = 0.5 * (LOW + HIGH)
    half = 0.5 * (HIGH - LOW)
    return [
        1.0 / (middle + half * math.cos(math.pi * (2 * j + 1) / (2 * count))) for j in range(count)
    ]


def power(x, count):
    result = None
    while count:
        if count & 1:
            result = x if result is None else result * x
        count >>= 1
        if count:
            x = x * x
    return result


def group_size(count):
    low = 1
    while low * low < count:
        low *= 2
    return low if count % low == 0 else count


def kernel(
    crosses, strikes, dips, pressure, facies, source, table, out_p, out_d, x, fac, halo, halo_fac,
    rims, mob, res, ans, part, qpow, full, col, rim_ans, rim_base, near_box, far_box, far_out,
    cross_sems, halo_sems, rim_sems, near_sems, far_sems, out_sems,
):
    tiles, width = x.shape[2], x.shape[4]
    main = width - LANES
    rows = tiles * SUB
    members = near_box.shape[1]
    groups = far_box.shape[1]
    cross = lax.axis_index("cross")
    strike = lax.axis_index("strike")
    member = lax.rem(strike, members)
    group = lax.div(strike, members)

    def across(k):
        return lax.rem(cross + k, crosses)

    def before(k):
        return lax.rem(cross + crosses - k, crosses)

    up = lax.rem(strike + 1, strikes)
    down = lax.rem(strike + strikes - 1, strikes)

    def near_peer(k):
        return (cross, group * members + lax.rem(member + k, members))

    def far_peer(k):
        return (cross, lax.rem(group + k, groups) * members + member)

    barrier = pltpu.get_barrier_semaphore()
    peers = [(across(k), strike) for k in range(1, crosses)]
    peers += [(cross, up), (cross, down)]
    peers += [near_peer(k) for k in range(1, members)]
    peers += [far_peer(k) for k in range(1, groups)]
    for peer in peers:
        pl.semaphore_signal(barrier, inc=1, device_id=peer, device_id_type=MESH)
    pl.semaphore_wait(barrier, len(peers))

    def send(src, dst, sems, where, target, k):
        if k == 0:
            return pltpu.make_async_copy(src, dst, sems.at[(1,) + where])
        return pltpu.make_async_remote_copy(
            src_ref=src,
            dst_ref=dst,
            send_sem=sems.at[(0,) + where],
            recv_sem=sems.at[(1,) + where],
            device_id=target,
            device_id_type=MESH,
        )

    def arrived(ref, sems, where, target, k):
        copy = send(ref, ref, sems, where, target, k)
        if k == 0:
            copy.wait()
        else:
            copy.wait_recv()

    def landing(f, c):
        if f == 1:
            return fac.at[c, :, :, pl.ds(0, main)], halo_fac.at[c]
        return x.at[c, f, :, :, pl.ds(0, main)], halo.at[c, f // 2]

    def columns(start, size):
        return pl.ds(pl.multiple_of(start, LANES), size)

    raws = (pressure, facies, source)
    for k in range(crosses):
        to = across(k)
        after = lax.rem(to + 1, crosses) * main
        ahead = lax.rem(to + crosses - 1, crosses) * main + main - LANES
        for f in range(3):
            body, edge = landing(f, cross)
            for t in range(tiles):
                send(
                    raws[f].at[:, t, 0, columns(to * main, main)], body.at[t],
                    cross_sems, (f, k), (to, strike), k,
                ).start()
            for t in range(tiles):
                for side, begin in ((0, after), (1, ahead)):
                    send(
                        raws[f].at[:, t, 0, columns(begin, LANES)], edge.at[side, t],
                        halo_sems, (f, k), (to, strike), k,
                    ).start()
    for k in range(crosses):
        for f in range(3):
            body, edge = landing(f, before(k))
            arrived(body, cross_sems, (f, k), (across(k), strike), k)
            arrived(edge, halo_sems, (f, k), (across(k), strike), k)

    inside = (strike > 0, strike < strikes - 1)
    lane = lax.broadcasted_iota(jnp.int32, (1, 1, width), 2)
    valid = (
        (lane < main)
        | ((lane < main + HALF) & (cross < crosses - 1))
        | ((lane >= main + HALF) & (cross > 0))
    )
    sub = lax.broadcasted_iota(jnp.int32, (crosses, SUB, width), 1)
    none = jnp.zeros((1, SUB, width), jnp.float32)
    tip = lax.broadcasted_iota(jnp.int32, (crosses, SUB, LANES), 2) < HALF
    real = valid[:, :, main:]

    def classed(codes):
        base = jnp.zeros(codes.shape, jnp.float32)
        for code in range(CLASSES):
            base = jnp.where(codes == code, table[code], base)
        return base

    for t in range(tiles):
        for f in (0, 2):
            merged = jnp.where(tip, halo[:, f // 2, 0, t], halo[:, f // 2, 1, t])
            x[:, f, t, :, main:] = jnp.where(real, merged, 0.0)
        merged = classed(jnp.where(tip, halo_fac[:, 0, t], halo_fac[:, 1, t]))
        x[:, 1, t, :, main:] = jnp.where(real, merged, 0.0)
        x[:, 1, t, :, :main] = classed(fac[:, t, :, :main])

    rim_copies = [
        send(
            x.at[:, pl.ds(0, 2), tile, pl.ds(row, 1), :], rims.at[side],
            rim_sems, (side,), (cross, target), 1,
        )
        for side, target, tile, row in ((0, up, tiles - 1, SUB - 1), (1, down, 0, 0))
    ]
    for copy in rim_copies:
        copy.start()

    def finals(which):
        ref = out_p if which == 0 else out_d
        copies = []
        for k in range(crosses):
            to = across(k)
            for t in range(tiles):
                src = x.at[to, 0, t] if which == 0 else res.at[to, t]
                copies.append(
                    send(
                        src.at[:, pl.ds(0, main)],
                        ref.at[:, t, 0, columns(cross * main, main)],
                        out_sems, (which, k), (to, strike), k,
                    )
                )
        return copies

    def left(a):
        return pltpu.roll(a, 1, 2)

    def right(a):
        return pltpu.roll(a, width - 1, 2)

    def later(a, k):
        return pltpu.roll(a, k, 1)

    def sooner(a, k):
        return pltpu.roll(a, SUB - k, 1)

    def mobility(base, p):
        return base * (1.0 + 0.5 * jnp.tanh(p))

    def trade(source, box, sems, count, peer_of, mine, parity):
        copies = []
        for k in range(1, count):
            copy = send(
                source(k), box(mine), sems, (parity, k - 1), peer_of(k), k
            )
            copy.start()
            copies.append(copy)

        def finish():
            for k in range(1, count):
                origin = lax.rem(mine + count - k, count)
                arrived(box(origin), sems, (parity, k - 1), peer_of(k), k)
            for copy in copies:
                copy.wait_send()

        return finish

    def trade_near(slots, parity):
        for i, slot in enumerate(slots):
            near_box[parity, member, i] = slot

        def box(a):
            return near_box.at[parity, a, pl.ds(0, len(slots))]

        return trade(lambda k: box(member), box, near_sems, members, near_peer, member, parity)

    def trade_far(upward, downward, parity):
        far_out[parity, 0] = upward
        far_out[parity, 1] = downward
        return trade(
            lambda k: far_out.at[parity, lax.div(group + k, groups)],
            lambda a: far_box.at[parity, a],
            far_sems, groups, far_peer, group, parity,
        )

    omega = chebyshev_weights(SWEEPS)

    def one_step(step, carry):
        turn = step * (SWEEPS + 1)
        parity = lax.rem(turn, 2)
        total = jnp.zeros((crosses, SUB, width), jnp.float32)
        for t in range(tiles):
            m = mobility(x[:, 1, t], x[:, 0, t])
            mob[t] = m
            total = total + m
        total = jnp.sum(total, axis=1, keepdims=True)
        finish = trade_near([total], parity)

        @pl.when(step == 0)
        def _():
            for copy in rim_copies:
                copy.wait_recv()
            for copy in rim_copies:
                copy.wait_send()
            for side in range(2):
                rim_ans[side, 1] = jnp.where(inside[side], rims[side, :, 0], 0.0)
                rim_base[side] = jnp.where(inside[side], rims[side, :, 1], 0.0)

        rim_p = [rim_ans[side, 1] for side in range(2)]
        rim_m = [mobility(rim_base[side], rim_p[side]) for side in range(2)]
        first_p, first_m = x[:, 0, 0], mob[0]
        last_p, last_m = x[:, 0, tiles - 1], mob[tiles - 1]
        p_was = jnp.where(sub == 0, rim_p[0], later(last_p, 1))
        m_was = jnp.where(sub == 0, rim_m[0], later(last_m, 1))
        p, m = first_p, first_m
        flux = 0.5 * (m + m_was) * (p - p_was)
        for t in range(tiles):
            if t + 1 < tiles:
                p_next, m_next = x[:, 0, t + 1], mob[t + 1]
            else:
                p_next = jnp.where(sub == SUB - 1, rim_p[1], sooner(first_p, 1))
                m_next = jnp.where(sub == SUB - 1, rim_m[1], sooner(first_m, 1))
            flux_next = 0.5 * (m_next + m) * (p_next - p)
            along = 0.5 * (m + left(m)) * (p - left(p))
            p_wide = jnp.concatenate([none, p, none], axis=0)
            m_wide = jnp.concatenate([none, m, none], axis=0)
            over = 0.5 * (m_wide[1:] + m_wide[:-1]) * (p_wide[1:] - p_wide[:-1])
            applied = STORE * p + (flux - flux_next) + (along - right(along)) + (over[:-1] - over[1:])
            res[:, t] = jnp.where(valid, x[:, 2, t] - applied, 0.0)
            ans[t] = jnp.zeros_like(p)
            p, m, flux = p_next, m_next, flux_next
            if t == tiles // 2 - 1:
                finish()
                total = near_box[parity, 0, 0]
                for a in range(1, members):
                    total = total + near_box[parity, a, 0]
                far_box[parity, group] = total
                finish = trade_far(total, total, parity)

        @pl.when(step == DEFECT - 1)
        def _():
            for copy in finals(1):
                copy.start()

        finish()
        total = far_box[parity, 0]
        for a in range(1, groups):
            total = total + far_box[parity, a]
        mref = total * (1.0 / dips)

        root = jnp.sqrt((STORE + 4.0 * mref) * (STORE + 8.0 * mref))
        q = 2.0 * mref / (STORE + 6.0 * mref + root)
        gain = 1.0 / root
        chunk = power(q, tiles)
        block = power(q, rows)
        cluster = power(block, members)
        whole = power(cluster, groups)
        unmirror = 1.0 / (1.0 - whole * whole)
        mirror_up = jnp.ones_like(q)
        mirror_down = mirror_up
        twice = cluster * cluster
        for a in range(groups - 1):
            mirror_up = jnp.where(a < group, mirror_up * twice, mirror_up)
            mirror_down = jnp.where(a < groups - 1 - group, mirror_down * twice, mirror_down)
        for i, value in enumerate((chunk, block, cluster, unmirror, mirror_up, mirror_down)):
            col[i] = value
        spread = (crosses, SUB, width)
        for i, value in enumerate((mref, q, gain)):
            full[i] = jnp.broadcast_to(value, spread)
        running = q
        for t in range(tiles):
            qpow[t] = jnp.broadcast_to(running, spread)
            running = running * q
        ahead = jnp.ones((crosses, SUB, width), jnp.float32)
        behind = ahead
        step_up = jnp.broadcast_to(chunk, ahead.shape)
        for bit in (1, 2, 4):
            ahead = jnp.where((sub & bit) != 0, ahead * step_up, ahead)
            behind = jnp.where((sub & bit) == 0, behind * step_up, behind)
            step_up = step_up * step_up
        part[0], part[1] = ahead, behind
        for side in range(2):
            rim_ans[side, 0] = jnp.zeros((crosses, 1, width), jnp.float32)

        def sweep(j, carry):
            parity = lax.rem(turn + 1 + j, 2)
            weight = jnp.float32(omega[0])
            for i in range(1, SWEEPS):
                weight = jnp.where(j == i, jnp.float32(omega[i]), weight)
            keep = 1.0 - weight
            mref, q, chunk = full[0], full[1], col[0]

            y = jnp.zeros((crosses, SUB, width), jnp.float32)
            for t in range(tiles):
                u = ans[t]
                near = left(u) + right(u)
                if crosses > 1:
                    near = near + jnp.concatenate([none, u[:-1]], axis=0)
                    near = near + jnp.concatenate([u[1:], none], axis=0)
                r = res[:, t] + mref * near
                mob[t] = r
                y = r + q * y
                qv = y - r
                part[2 + t] = qv
            z = jnp.zeros((crosses, SUB, width), jnp.float32)
            for t in reversed(range(tiles)):
                z = mob[t] + q * z
                part[2 + t] = part[2 + t] + z
            step_up = chunk
            for k in (1, 2, 4):
                y = y + step_up * jnp.where(sub >= k, later(y, k), 0.0)
                z = z + step_up * jnp.where(sub < SUB - k, sooner(z, k), 0.0)
                step_up = step_up * step_up
            tail, head = y[:, SUB - 1 :, :], z[:, :1, :]
            trade_near([tail, head], parity)()

            block, cluster, unmirror = col[1], col[2], col[3]
            fore = near_box[parity, 0, 0]
            back = near_box[parity, members - 1, 1]
            for a in range(1, members):
                fore = fore * block + near_box[parity, a, 0]
                back = back * block + near_box[parity, members - 1 - a, 1]
            mirror_up, mirror_down = col[4], col[5]
            upward = fore + mirror_up * cluster * back
            downward = back + mirror_down * cluster * fore
            trade_far(upward, downward, parity)()
            from_left = jnp.zeros_like(upward)
            from_right = jnp.zeros_like(upward)
            for a in range(groups - 1):
                b = groups - 1 - a
                from_left = jnp.where(
                    a < group, from_left * cluster + far_box[parity, a], from_left
                )
                from_right = jnp.where(
                    b > group, from_right * cluster + far_box[parity, b], from_right
                )
            from_left, from_right = (
                (from_left + mirror_up * (from_right * cluster + downward)) * unmirror,
                (from_right + mirror_down * (from_left * cluster + upward)) * unmirror,
            )
            for a in range(members - 1):
                b = members - 1 - a
                from_left = jnp.where(
                    a < member, from_left * block + near_box[parity, a, 0], from_left
                )
                from_right = jnp.where(
                    b > member, from_right * block + near_box[parity, b, 1], from_right
                )

            thin_q = q[:, :1, :]
            scale = weight * full[2]
            thin_scale = scale[:, :1, :]
            rim_ans[0, 0] = keep * rim_ans[0, 0] + thin_scale * (
                from_left + thin_q * (head + block * from_right)
            )
            rim_ans[1, 0] = keep * rim_ans[1, 0] + thin_scale * (
                from_right + thin_q * (tail + block * from_left)
            )
            y = jnp.where(sub >= 1, later(y, 1), 0.0) + part[0] * from_left
            z = jnp.where(sub < SUB - 1, sooner(z, 1), 0.0) + part[1] * from_right
            for t in range(tiles):
                solved = part[2 + t] + qpow[t] * y + qpow[tiles - 1 - t] * z
                ans[t] = keep * ans[t] + scale * solved
            return carry

        lax.fori_loop(0, SWEEPS, sweep, 0)
        for t in range(tiles):
            x[:, 0, t] = x[:, 0, t] + ans[t]
        for side in range(2):
            rim_ans[side, 1] = rim_ans[side, 1] + jnp.where(inside[side], rim_ans[side, 0], 0.0)
        return carry

    lax.fori_loop(0, DEFECT, one_step, 0)

    for copy in finals(0):
        copy.start()
    for which in (1, 0):
        ref = out_p if which == 0 else out_d
        for k in range(crosses):
            to, frm = across(k), before(k)
            arrived(
                ref.at[:, :, 0, columns(frm * main, main)], out_sems, (which, k), (to, strike), k
            )
    for k in range(1, crosses):
        to = across(k)
        for f in range(3):
            body, edge = landing(f, cross)
            send(body, body, cross_sems, (f, k), (to, strike), k).wait_send()
            send(edge, edge, halo_sems, (f, k), (to, strike), k).wait_send()
        for which in range(2):
            src = x.at[to, 0] if which == 0 else res.at[to]
            src = src.at[:, :, pl.ds(0, main)]
            send(src, src, out_sems, (which, k), (to, strike), k).wait_send()


def per_device(pressure, source, facies, mobility_table):
    crosses = lax.axis_size("cross")
    strikes = lax.axis_size("strike")
    rows, _, cells = pressure.shape
    tiles = rows // SUB
    main = cells // crosses
    width = main + LANES
    members = group_size(strikes)
    groups = strikes // members

    def dealt(a):
        return a.reshape(SUB, tiles, 1, cells)

    f32 = jnp.float32
    vm = pltpu.VMEM
    dma = pltpu.SemaphoreType.DMA
    full = (crosses, SUB, width)
    field = (tiles,) + full
    thin = (crosses, 1, width)
    whole = jax.ShapeDtypeStruct((SUB, tiles, 1, cells), f32)
    anywhere = pl.BlockSpec(memory_space=pl.ANY)
    outs = pl.pallas_call(
        functools.partial(kernel, crosses, strikes, rows * strikes),
        out_shape=[whole, whole],
        in_specs=[anywhere] * 3 + [pl.BlockSpec(memory_space=pltpu.SMEM)],
        out_specs=[anywhere] * 2,
        scratch_shapes=[
            vm((crosses, 3, tiles, SUB, width), f32),
            vm((crosses, tiles, SUB, width), jnp.int32),
            vm((crosses, 2, 2, tiles, SUB, LANES), f32),
            vm((crosses, 2, tiles, SUB, LANES), jnp.int32),
            vm((2, crosses, 2, 1, width), f32),
            vm(field, f32),
            vm((crosses, tiles, SUB, width), f32),
            vm(field, f32),
            vm((tiles + 2,) + full, f32),
            vm(field, f32),
            vm((3,) + full, f32),
            vm((6,) + thin, f32),
            vm((2, 2) + thin, f32),
            vm((2,) + thin, f32),
            vm((2, members, 2) + thin, f32),
            vm((2, groups) + thin, f32),
            vm((2, 2) + thin, f32),
            dma((2, 3, crosses)),
            dma((2, 3, crosses)),
            dma((2, 2)),
            dma((2, 2, max(members - 1, 1))),
            dma((2, 2, max(groups - 1, 1))),
            dma((2, 2, crosses)),
        ],
        compiler_params=pltpu.CompilerParams(
            collective_id=0, has_side_effects=True, vmem_limit_bytes=40 * 1024 * 1024
        ),
    )(dealt(pressure), dealt(facies), dealt(source), mobility_table)
    return tuple(a.reshape(rows, 1, cells) for a in outs)


def solution(mesh):
    in_specs = (
        P("strike", "cross", None),
        P("strike", "cross", None),
        P("strike", "cross", None),
        P(),
    )
    out_specs = (P("strike", "cross", None), P("strike", "cross", None))
    return jax.shard_map(
        per_device, mesh=mesh, in_specs=in_specs, out_specs=out_specs, check_vma=False
    )
```

time: 90.5 us -> 79.7 us (0.88)
  other arithmetic: 6.9 us -> 0 us
  local copies, waits for them, and re-layouts: 7.33 us -> 5.36 us
  Pallas kernels: 75.2 us -> 73.4 us
    reshape x1 -> x0, other arithmetic: 6.47 us -> none  [dealt(): return a.reshape(SUB, tiles, cells).transpose(1, 0, 2)]
    unnamed x6 -> x10, local copies, waits for them, and re-layouts: 0.56 us -> 5.36 us
    reshape x5 -> x0, local copies, waits for them, and re-layouts: 4.13 us -> none  [the longest x2 3.21 us: gathered(): return a.transpose(2, 1, 0, 3).reshape(rows, 1, cells)]
    pallas_call x1, Pallas kernels: 75.2 us -> 73.4 us  [per_device(): pl.pallas_call(functools.partial(kernel, crosses, strikes, rows * strikes...]
    slice x2 -> x0, local copies, waits for them, and re-layouts: 1.74 us -> none  [the longest x1 1.64 us: lookup(): base = jnp.where(classes == code, table[code], base)]
where the time goes in v2:
time: 79.7 us; the launch traced here: 79.4 us
  Pallas kernels  73.4 us (92%)
  local copies, waits for them, and re-layouts  5.36 us (7%)
    pallas_call x1, Pallas kernels, per_device(): pl.pallas_call(functools.partial(kernel, crosses, strikes, rows * strikes...  73.4 us
    unnamed x10, local copies, waits for them, and re-layouts  5.36 us

profile of v2, /device:TPU:0, one launch (start us, length us, event | category | flops | bytes accessed | tf_op | source)
XLA Modules:
  0.0 79.4 jit_solution(16573591246434187876)
XLA Ops:
  0.6 0.0 copy-start.3
  0.6 0.6 copy-done.3
  1.3 0.0 copy-start
  1.3 1.0 %copy-done = f32[64,1,2048]{2,1,0:T(1,128)S(1)} copy-done((f32[64,1,2048]{2,1,0:T(1,128)S(1)}, f32[64,1,2048]{2,1,0:T(1,128)}, u32[]{:S(2)}) %copy-start) | copy-done | bytes 524312
  2.3 0.0 copy-start.1
  2.3 1.0 %copy-done.1 = s32[64,1,2048]{2,1,0:T(1,128)S(1)} copy-done((s32[64,1,2048]{2,1,0:T(1,128)S(1)}, s32[64,1,2048]{2,1,0:T(1,128)}, u32[]{:S(2)}) %copy-start.1) | copy-done | bytes 524312
  3.4 0.0 copy-start.2
  3.4 1.0 %copy-done.2 = f32[64,1,2048]{2,1,0:T(1,128)S(1)} copy-done((f32[64,1,2048]{2,1,0:T(1,128)S(1)}, f32[64,1,2048]{2,1,0:T(1,128)}, u32[]{:S(2)}) %copy-start.2) | copy-done | bytes 524312
  4.4 73.4 %shard_map.59 = (f32[8,8,1,2048]{3,2,1,0:T(1,128)S(1)}, f32[8,8,1,2048]{3,2,1,0:T(1,128)S(1)}) custom-call(f32[8,8,1,2048]{3,2,1,0:T(1,128)S(1)} %bitcast.5, s32[8,8,1,2048]{3,2,1,0:T(1,128)S(1)} %bitcast.6, f32[8,8,1,2048]{3,2,1,0:T(1,128)S(1)} %bitcast.7, f32[8]{0:T(128)S(1)} %copy-done.3), custom_call_target="tpu_custom_call" | custom-call | tf_op jit(solution)/shard_map/pallas_call | solution.py:475
  77.9 0.8 %copy.8 = f32[64,1,2048]{2,1,0:T(1,128)} copy(f32[64,1,2048]{2,1,0:T(1,128)S(1)} %bitcast.9) | data formatting | bytes 1048576
  78.7 0.8 copy.9
Async XLA Ops:
  0.6 0.7 copy-start.3
  1.3 1.0 %copy-start = (f32[64,1,2048]{2,1,0:T(1,128)S(1)}, f32[64,1,2048]{2,1,0:T(1,128)}, u32[]{:S(2)}) copy-start(f32[64,1,2048]{2,1,0:T(1,128)} %param.4) | copy-start | bytes 1572868
  2.3 1.0 %copy-start.1 = (s32[64,1,2048]{2,1,0:T(1,128)S(1)}, s32[64,1,2048]{2,1,0:T(1,128)}, u32[]{:S(2)}) copy-start(s32[64,1,2048]{2,1,0:T(1,128)} %param.6) | copy-start | bytes 1572868
  3.4 1.0 %copy-start.2 = (f32[64,1,2048]{2,1,0:T(1,128)S(1)}, f32[64,1,2048]{2,1,0:T(1,128)}, u32[]{:S(2)}) copy-start(f32[64,1,2048]{2,1,0:T(1,128)} %param.5) | copy-start | bytes 1572868

commit v3 on v2

--- a/solution.py
+++ b/solution.py
@@ -39,13 +39,6 @@
         if count:
             x = x * x
     return result
-
-
-def group_size(count):
-    low = 1
-    while low * low < count:
-        low *= 2
-    return low if count % low == 0 else count
 
 
 def kernel(
@@ -458,7 +451,7 @@
     tiles = rows // SUB
     main = cells // crosses
     width = main + LANES
-    members = group_size(strikes)
+    members = 1
     groups = strikes // members
 
     def dealt(a):
@@ -471,7 +464,7 @@
     field = (tiles,) + full
     thin = (crosses, 1, width)
     whole = jax.ShapeDtypeStruct((SUB, tiles, 1, cells), f32)
-    anywhere = pl.BlockSpec(memory_space=pl.ANY)
+    anywhere = pl.BlockSpec(memory_space=pltpu.HBM)
     outs = pl.pallas_call(
         functools.partial(kernel, crosses, strikes, rows * strikes),
         out_shape=[whole, whole],

time: 79.7 us -> 72 us (0.903)
  Pallas kernels: 73.4 us -> 65.7 us
    pallas_call x1, Pallas kernels: 73.4 us -> 65.7 us  [per_device(): pl.pallas_call(functools.partial(kernel, crosses, strikes, rows * strikes...]
where the time goes in v3:
time: 72 us; the launch traced here: 71.7 us
  Pallas kernels  65.7 us (91%)
  local copies, waits for them, and re-layouts  5.36 us (7%)
    pallas_call x1, Pallas kernels, per_device(): pl.pallas_call(functools.partial(kernel, crosses, strikes, rows * strikes...  65.7 us
    unnamed x10, local copies, waits for them, and re-layouts  5.36 us

profile of v3, /device:TPU:0, one launch (start us, length us, event | category | flops | bytes accessed | tf_op | source)
XLA Modules:
  0.0 71.7 jit_solution(2562874252975455093)
XLA Ops:
  0.6 0.0 copy-start.3
  0.6 0.6 copy-done.3
  1.3 0.0 copy-start
  1.3 1.0 %copy-done = f32[64,1,2048]{2,1,0:T(1,128)S(1)} copy-done((f32[64,1,2048]{2,1,0:T(1,128)S(1)}, f32[64,1,2048]{2,1,0:T(1,128)}, u32[]{:S(2)}) %copy-start) | copy-done | bytes 524312
  2.3 0.0 copy-start.1
  2.3 1.0 %copy-done.1 = s32[64,1,2048]{2,1,0:T(1,128)S(1)} copy-done((s32[64,1,2048]{2,1,0:T(1,128)S(1)}, s32[64,1,2048]{2,1,0:T(1,128)}, u32[]{:S(2)}) %copy-start.1) | copy-done | bytes 524312
  3.4 0.0 copy-start.2
  3.4 1.0 %copy-done.2 = f32[64,1,2048]{2,1,0:T(1,128)S(1)} copy-done((f32[64,1,2048]{2,1,0:T(1,128)S(1)}, f32[64,1,2048]{2,1,0:T(1,128)}, u32[]{:S(2)}) %copy-start.2) | copy-done | bytes 524312
  4.4 65.7 %shard_map.59 = (f32[8,8,1,2048]{3,2,1,0:T(1,128)S(1)}, f32[8,8,1,2048]{3,2,1,0:T(1,128)S(1)}) custom-call(f32[8,8,1,2048]{3,2,1,0:T(1,128)S(1)} %bitcast.5, s32[8,8,1,2048]{3,2,1,0:T(1,128)S(1)} %bitcast.6, f32[8,8,1,2048]{3,2,1,0:T(1,128)S(1)} %bitcast.7, f32[8]{0:T(128)S(1)} %copy-done.3), custom_call_target="tpu_custom_call" | custom-call | tf_op jit(solution)/shard_map/pallas_call | solution.py:468
  70.1 0.8 %copy.8 = f32[64,1,2048]{2,1,0:T(1,128)} copy(f32[64,1,2048]{2,1,0:T(1,128)S(1)} %bitcast.9) | data formatting | bytes 1048576
  70.9 0.8 %copy.9 = f32[64,1,2048]{2,1,0:T(1,128)} copy(f32[64,1,2048]{2,1,0:T(1,128)S(1)} %bitcast.8) | data formatting | bytes 1048576
Async XLA Ops:
  0.6 0.7 copy-start.3
  1.3 1.0 %copy-start = (f32[64,1,2048]{2,1,0:T(1,128)S(1)}, f32[64,1,2048]{2,1,0:T(1,128)}, u32[]{:S(2)}) copy-start(f32[64,1,2048]{2,1,0:T(1,128)} %param.4) | copy-start | bytes 1572868
  2.3 1.0 %copy-start.1 = (s32[64,1,2048]{2,1,0:T(1,128)S(1)}, s32[64,1,2048]{2,1,0:T(1,128)}, u32[]{:S(2)}) copy-start(s32[64,1,2048]{2,1,0:T(1,128)} %param.6) | copy-start | bytes 1572868
  3.4 1.0 %copy-start.2 = (f32[64,1,2048]{2,1,0:T(1,128)S(1)}, f32[64,1,2048]{2,1,0:T(1,128)}, u32[]{:S(2)}) copy-start(f32[64,1,2048]{2,1,0:T(1,128)} %param.5) | copy-start | bytes 1572868

commit v4 on v3

--- a/solution.py
+++ b/solution.py
@@ -43,18 +43,16 @@
 
 def kernel(
     crosses, strikes, dips, pressure, facies, source, table, out_p, out_d, x, fac, halo, halo_fac,
-    rims, mob, res, ans, part, qpow, full, col, rim_ans, rim_base, near_box, far_box, far_out,
-    cross_sems, halo_sems, rim_sems, near_sems, far_sems, out_sems,
+    rims, mob, res, ans, part, qpow, full, col, rim_ans, rim_base, far_box, far_out,
+    cross_sems, halo_sems, rim_sems, far_sems, out_sems,
 ):
     tiles, width = x.shape[2], x.shape[4]
     main = width - LANES
     rows = tiles * SUB
-    members = near_box.shape[1]
-    groups = far_box.shape[1]
+    pieces = 2 if crosses % 2 == 0 else 1
+    piece = crosses // pieces
     cross = lax.axis_index("cross")
     strike = lax.axis_index("strike")
-    member = lax.rem(strike, members)
-    group = lax.div(strike, members)
 
     def across(k):
         return lax.rem(cross + k, crosses)
@@ -65,17 +63,13 @@
     up = lax.rem(strike + 1, strikes)
     down = lax.rem(strike + strikes - 1, strikes)
 
-    def near_peer(k):
-        return (cross, group * members + lax.rem(member + k, members))
-
-    def far_peer(k):
-        return (cross, lax.rem(group + k, groups) * members + member)
+    def peer_of(k):
+        return (cross, lax.rem(strike + k, strikes))
 
     barrier = pltpu.get_barrier_semaphore()
     peers = [(across(k), strike) for k in range(1, crosses)]
     peers += [(cross, up), (cross, down)]
-    peers += [near_peer(k) for k in range(1, members)]
-    peers += [far_peer(k) for k in range(1, groups)]
+    peers += [peer_of(k) for k in range(1, strikes)]
     for peer in peers:
         pl.semaphore_signal(barrier, inc=1, device_id=peer, device_id_type=MESH)
     pl.semaphore_wait(barrier, len(peers))
@@ -138,7 +132,7 @@
         | ((lane < main + HALF) & (cross < crosses - 1))
         | ((lane >= main + HALF) & (cross > 0))
     )
-    sub = lax.broadcasted_iota(jnp.int32, (crosses, SUB, width), 1)
+    sub = lax.broadcasted_iota(jnp.int32, (1, SUB, width), 1)
     none = jnp.zeros((1, SUB, width), jnp.float32)
     tip = lax.broadcasted_iota(jnp.int32, (crosses, SUB, LANES), 2) < HALF
     real = valid[:, :, main:]
@@ -198,41 +192,27 @@
     def mobility(base, p):
         return base * (1.0 + 0.5 * jnp.tanh(p))
 
-    def trade(source, box, sems, count, peer_of, mine, parity):
+    def trade(parity, which, low, size):
+        def box(a):
+            return far_box.at[parity, a, pl.ds(low, size)]
+
         copies = []
-        for k in range(1, count):
-            copy = send(
-                source(k), box(mine), sems, (parity, k - 1), peer_of(k), k
-            )
+        for k in range(1, strikes):
+            row = far_out.at[parity, lax.div(strike + k, strikes), pl.ds(low, size)]
+            copy = send(row, box(strike), far_sems, (parity, which, k - 1), peer_of(k), k)
             copy.start()
             copies.append(copy)
 
         def finish():
-            for k in range(1, count):
-                origin = lax.rem(mine + count - k, count)
-                arrived(box(origin), sems, (parity, k - 1), peer_of(k), k)
+            for k in range(1, strikes):
+                origin = lax.rem(strike + strikes - k, strikes)
+                arrived(box(origin), far_sems, (parity, which, k - 1), peer_of(k), k)
+
+        def settle():
             for copy in copies:
                 copy.wait_send()
 
-        return finish
-
-    def trade_near(slots, parity):
-        for i, slot in enumerate(slots):
-            near_box[parity, member, i] = slot
-
-        def box(a):
-            return near_box.at[parity, a, pl.ds(0, len(slots))]
-
-        return trade(lambda k: box(member), box, near_sems, members, near_peer, member, parity)
-
-    def trade_far(upward, downward, parity):
-        far_out[parity, 0] = upward
-        far_out[parity, 1] = downward
-        return trade(
-            lambda k: far_out.at[parity, lax.div(group + k, groups)],
-            lambda a: far_box.at[parity, a],
-            far_sems, groups, far_peer, group, parity,
-        )
+        return finish, settle
 
     omega = chebyshev_weights(SWEEPS)
 
@@ -245,7 +225,10 @@
             mob[t] = m
             total = total + m
         total = jnp.sum(total, axis=1, keepdims=True)
-        finish = trade_near([total], parity)
+        far_out[parity, 0] = total
+        far_out[parity, 1] = total
+        far_box[parity, strike] = total
+        finish, settle = trade(parity, 0, 0, crosses)
 
         @pl.when(step == 0)
         def _():
@@ -280,13 +263,6 @@
             res[:, t] = jnp.where(valid, x[:, 2, t] - applied, 0.0)
             ans[t] = jnp.zeros_like(p)
             p, m, flux = p_next, m_next, flux_next
-            if t == tiles // 2 - 1:
-                finish()
-                total = near_box[parity, 0, 0]
-                for a in range(1, members):
-                    total = total + near_box[parity, a, 0]
-                far_box[parity, group] = total
-                finish = trade_far(total, total, parity)
 
         @pl.when(step == DEFECT - 1)
         def _():
@@ -294,8 +270,9 @@
                 copy.start()
 
         finish()
+        settle()
         total = far_box[parity, 0]
-        for a in range(1, groups):
+        for a in range(1, strikes):
             total = total + far_box[parity, a]
         mref = total * (1.0 / dips)
 
@@ -304,16 +281,15 @@
         gain = 1.0 / root
         chunk = power(q, tiles)
         block = power(q, rows)
-        cluster = power(block, members)
-        whole = power(cluster, groups)
+        whole = power(block, strikes)
         unmirror = 1.0 / (1.0 - whole * whole)
         mirror_up = jnp.ones_like(q)
         mirror_down = mirror_up
-        twice = cluster * cluster
-        for a in range(groups - 1):
-            mirror_up = jnp.where(a < group, mirror_up * twice, mirror_up)
-            mirror_down = jnp.where(a < groups - 1 - group, mirror_down * twice, mirror_down)
-        for i, value in enumerate((chunk, block, cluster, unmirror, mirror_up, mirror_down)):
+        twice = block * block
+        for a in range(strikes - 1):
+            mirror_up = jnp.where(a < strike, mirror_up * twice, mirror_up)
+            mirror_down = jnp.where(a < strikes - 1 - strike, mirror_down * twice, mirror_down)
+        for i, value in enumerate((chunk, block, unmirror, mirror_up, mirror_down)):
             col[i] = value
         spread = (crosses, SUB, width)
         for i, value in enumerate((mref, q, gain)):
@@ -339,79 +315,82 @@
             for i in range(1, SWEEPS):
                 weight = jnp.where(j == i, jnp.float32(omega[i]), weight)
             keep = 1.0 - weight
-            mref, q, chunk = full[0], full[1], col[0]
-
-            y = jnp.zeros((crosses, SUB, width), jnp.float32)
-            for t in range(tiles):
-                u = ans[t]
-                near = left(u) + right(u)
-                if crosses > 1:
-                    near = near + jnp.concatenate([none, u[:-1]], axis=0)
-                    near = near + jnp.concatenate([u[1:], none], axis=0)
-                r = res[:, t] + mref * near
-                mob[t] = r
-                y = r + q * y
-                qv = y - r
-                part[2 + t] = qv
-            z = jnp.zeros((crosses, SUB, width), jnp.float32)
-            for t in reversed(range(tiles)):
-                z = mob[t] + q * z
-                part[2 + t] = part[2 + t] + z
-            step_up = chunk
-            for k in (1, 2, 4):
-                y = y + step_up * jnp.where(sub >= k, later(y, k), 0.0)
-                z = z + step_up * jnp.where(sub < SUB - k, sooner(z, k), 0.0)
-                step_up = step_up * step_up
-            tail, head = y[:, SUB - 1 :, :], z[:, :1, :]
-            trade_near([tail, head], parity)()
-
-            block, cluster, unmirror = col[1], col[2], col[3]
-            fore = near_box[parity, 0, 0]
-            back = near_box[parity, members - 1, 1]
-            for a in range(1, members):
-                fore = fore * block + near_box[parity, a, 0]
-                back = back * block + near_box[parity, members - 1 - a, 1]
-            mirror_up, mirror_down = col[4], col[5]
-            upward = fore + mirror_up * cluster * back
-            downward = back + mirror_down * cluster * fore
-            trade_far(upward, downward, parity)()
-            from_left = jnp.zeros_like(upward)
-            from_right = jnp.zeros_like(upward)
-            for a in range(groups - 1):
-                b = groups - 1 - a
-                from_left = jnp.where(
-                    a < group, from_left * cluster + far_box[parity, a], from_left
+            waiting = []
+            for which in range(pieces):
+                low, high = which * piece, (which + 1) * piece
+                mref, q, chunk = full[0, low:high], full[1, low:high], col[0, low:high]
+                y = jnp.zeros((piece, SUB, width), jnp.float32)
+                for t in range(tiles):
+                    u = ans[t, low:high]
+                    near = left(u) + right(u)
+                    if low > 0:
+                        near = near + ans[t, low - 1 : high - 1]
+                    elif piece > 1:
+                        near = near + jnp.concatenate([none, u[:-1]], axis=0)
+                    if high < crosses:
+                        near = near + ans[t, low + 1 : high + 1]
+                    elif piece > 1:
+                        near = near + jnp.concatenate([u[1:], none], axis=0)
+                    r = res[low:high, t] + mref * near
+                    mob[t, low:high] = r
+                    y = q * y
+                    part[2 + t, low:high] = y
+                    y = r + y
+                z = jnp.zeros((piece, SUB, width), jnp.float32)
+                for t in reversed(range(tiles)):
+                    z = mob[t, low:high] + q * z
+                    part[2 + t, low:high] = part[2 + t, low:high] + z
+                step_up = chunk
+                for k in (1, 2, 4):
+                    y = y + step_up * jnp.where(sub >= k, later(y, k), 0.0)
+                    z = z + step_up * jnp.where(sub < SUB - k, sooner(z, k), 0.0)
+                    step_up = step_up * step_up
+                tail, head = y[:, SUB - 1 :, :], z[:, :1, :]
+                block = col[1, low:high]
+                far_out[parity, 0, low:high] = tail + col[3, low:high] * block * head
+                far_out[parity, 1, low:high] = head + col[4, low:high] * block * tail
+                waiting.append((y, z, tail, head) + trade(parity, which, low, piece))
+
+            for which in range(pieces):
+                low, high = which * piece, (which + 1) * piece
+                y, z, tail, head, finish, settle = waiting[which]
+                block, unmirror = col[1, low:high], col[2, low:high]
+                mirror_up, mirror_down = col[3, low:high], col[4, low:high]
+                thin_q = full[1, low:high, :1, :]
+                scale = weight * full[2, low:high]
+                thin_scale = weight * full[2, low:high, :1, :]
+                upward = far_out[parity, 0, low:high]
+                downward = far_out[parity, 1, low:high]
+                finish()
+                from_left = jnp.zeros_like(upward)
+                from_right = jnp.zeros_like(upward)
+                for a in range(strikes - 1):
+                    b = strikes - 1 - a
+                    from_left = jnp.where(
+                        a < strike, from_left * block + far_box[parity, a, low:high], from_left
+                    )
+                    from_right = jnp.where(
+                        b > strike, from_right * block + far_box[parity, b, low:high], from_right
+                    )
+                from_left, from_right = (
+                    (from_left + mirror_up * (from_right * block + downward)) * unmirror,
+                    (from_right + mirror_down * (from_left * block + upward)) * unmirror,
                 )
-                from_right = jnp.where(
-                    b > group, from_right * cluster + far_box[parity, b], from_right
+                rim_ans[0, 0, low:high] = keep * rim_ans[0, 0, low:high] + thin_scale * (
+                    from_left + thin_q * (head + block * from_right)
                 )
-            from_left, from_right = (
-                (from_left + mirror_up * (from_right * cluster + downward)) * unmirror,
-                (from_right + mirror_down * (from_left * cluster + upward)) * unmirror,
-            )
-            for a in range(members - 1):
-                b = members - 1 - a
-                from_left = jnp.where(
-                    a < member, from_left * block + near_box[parity, a, 0], from_left
+                rim_ans[1, 0, low:high] = keep * rim_ans[1, 0, low:high] + thin_scale * (
+                    from_right + thin_q * (tail + block * from_left)
                 )
-                from_right = jnp.where(
-                    b > member, from_right * block + near_box[parity, b, 1], from_right
-                )
-
-            thin_q = q[:, :1, :]
-            scale = weight * full[2]
-            thin_scale = scale[:, :1, :]
-            rim_ans[0, 0] = keep * rim_ans[0, 0] + thin_scale * (
-                from_left + thin_q * (head + block * from_right)
-            )
-            rim_ans[1, 0] = keep * rim_ans[1, 0] + thin_scale * (
-                from_right + thin_q * (tail + block * from_left)
-            )
-            y = jnp.where(sub >= 1, later(y, 1), 0.0) + part[0] * from_left
-            z = jnp.where(sub < SUB - 1, sooner(z, 1), 0.0) + part[1] * from_right
-            for t in range(tiles):
-                solved = part[2 + t] + qpow[t] * y + qpow[tiles - 1 - t] * z
-                ans[t] = keep * ans[t] + scale * solved
+                y = jnp.where(sub >= 1, later(y, 1), 0.0) + part[0, low:high] * from_left
+                z = jnp.where(sub < SUB - 1, sooner(z, 1), 0.0) + part[1, low:high] * from_right
+                for t in range(tiles):
+                    solved = part[2 + t, low:high] + (
+                        qpow[t, low:high] * y + qpow[tiles - 1 - t, low:high] * z
+                    )
+                    ans[t, low:high] = keep * ans[t, low:high] + scale * solved
+            for which in range(pieces):
+                waiting[which][5]()
             return carry
 
         lax.fori_loop(0, SWEEPS, sweep, 0)
@@ -451,8 +430,6 @@
     tiles = rows // SUB
     main = cells // crosses
     width = main + LANES
-    members = 1
-    groups = strikes // members
 
     def dealt(a):
         return a.reshape(SUB, tiles, 1, cells)
@@ -482,21 +459,19 @@
             vm((tiles + 2,) + full, f32),
             vm(field, f32),
             vm((3,) + full, f32),
-            vm((6,) + thin, f32),
+            vm((5,) + thin, f32),
             vm((2, 2) + thin, f32),
             vm((2,) + thin, f32),
-            vm((2, members, 2) + thin, f32),
-            vm((2, groups) + thin, f32),
+            vm((2, strikes) + thin, f32),
             vm((2, 2) + thin, f32),
             dma((2, 3, crosses)),
             dma((2, 3, crosses)),
             dma((2, 2)),
-            dma((2, 2, max(members - 1, 1))),
-            dma((2, 2, max(groups - 1, 1))),
+            dma((2, 2, 2, max(strikes - 1, 1))),
             dma((2, 2, crosses)),
         ],
         compiler_params=pltpu.CompilerParams(
-            collective_id=0, has_side_effects=True, vmem_limit_bytes=40 * 1024 * 1024
+            collective_id=0, has_side_effects=True, vmem_limit_bytes=60 * 1024 * 1024
         ),
     )(dealt(pressure), dealt(facies), dealt(source), mobility_table)
     return tuple(a.reshape(rows, 1, cells) for a in outs)

time: 72 us -> 65.8 us (0.914)
  Pallas kernels: 65.7 us -> 62.2 us
  local copies, waits for them, and re-layouts: 5.36 us -> 2.72 us
    pallas_call x1, Pallas kernels: 65.7 us -> 62.2 us  [per_device(): pl.pallas_call(functools.partial(kernel, crosses, strikes, rows * strikes...]
    unnamed x10 -> x4, local copies, waits for them, and re-layouts: 5.36 us -> 2.72 us
where the time goes in v4:
time: 65.8 us; the launch traced here: 65.6 us
  Pallas kernels  62.2 us (95%)
  local copies, waits for them, and re-layouts  2.72 us (4%)
    pallas_call x1, Pallas kernels, per_device(): pl.pallas_call(functools.partial(kernel, crosses, strikes, rows * strikes...  62.2 us
    unnamed x4, local copies, waits for them, and re-layouts  2.72 us

profile of v4, /device:TPU:0, one launch (start us, length us, event | category | flops | bytes accessed | tf_op | source)
XLA Modules:
  0.0 65.6 jit_solution(4963202690664546682)
XLA Ops:
  0.6 62.2 %shard_map.59 = (f32[8,8,1,2048]{3,2,1,0:T(1,128)}, f32[8,8,1,2048]{3,2,1,0:T(1,128)}) custom-call(f32[8,8,1,2048]{3,2,1,0:T(1,128)} %bitcast.5, s32[8,8,1,2048]{3,2,1,0:T(1,128)} %bitcast.6, f32[8,8,1,2048]{3,2,1,0:T(1,128)} %bitcast.7, f32[8]{0:T(128)} %table.1), custom_call_target="tpu_custom_call" | custom-call | tf_op jit(solution)/shard_map/pallas_call | solution.py:445
  62.8 0.0 copy-start
  62.8 1.9 %copy.8 = f32[64,1,2048]{2,1,0:T(1,128)} copy(f32[64,1,2048]{2,1,0:T(1,128)} %bitcast.9) | data formatting | bytes 1048576
  64.8 0.0 copy-done
  64.8 0.8 %copy.9 = f32[64,1,2048]{2,1,0:T(1,128)} copy(f32[64,1,2048]{2,1,0:T(1,128)S(1)} %bitcast.8) | data formatting | bytes 1048576
Async XLA Ops:
  62.8 1.9 %copy-start = (f32[8,8,1,2048]{3,2,1,0:T(1,128)S(1)}, f32[8,8,1,2048]{3,2,1,0:T(1,128)}, u32[]{:S(2)}) copy-start(f32[8,8,1,2048]{3,2,1,0:T(1,128)} %get-tuple-element.5) | copy-start | bytes 1572868

commit v5 on v4

--- a/solution.py
+++ b/solution.py
@@ -72,7 +72,6 @@
     peers += [peer_of(k) for k in range(1, strikes)]
     for peer in peers:
         pl.semaphore_signal(barrier, inc=1, device_id=peer, device_id_type=MESH)
-    pl.semaphore_wait(barrier, len(peers))
 
     def send(src, dst, sems, where, target, k):
         if k == 0:
@@ -102,7 +101,8 @@
         return pl.ds(pl.multiple_of(start, LANES), size)
 
     raws = (pressure, facies, source)
-    for k in range(crosses):
+
+    def deal(k):
         to = across(k)
         after = lax.rem(to + 1, crosses) * main
         ahead = lax.rem(to + crosses - 1, crosses) * main + main - LANES
@@ -119,11 +119,19 @@
                         raws[f].at[:, t, 0, columns(begin, LANES)], edge.at[side, t],
                         halo_sems, (f, k), (to, strike), k,
                     ).start()
-    for k in range(crosses):
-        for f in range(3):
+
+    def dealt(f):
+        for k in range(crosses):
             body, edge = landing(f, before(k))
             arrived(body, cross_sems, (f, k), (across(k), strike), k)
             arrived(edge, halo_sems, (f, k), (across(k), strike), k)
+
+    deal(0)
+    pl.semaphore_wait(barrier, len(peers))
+    for k in range(1, crosses):
+        deal(k)
+    dealt(0)
+    dealt(1)
 
     inside = (strike > 0, strike < strikes - 1)
     lane = lax.broadcasted_iota(jnp.int32, (1, 1, width), 2)
@@ -143,10 +151,13 @@
             base = jnp.where(codes == code, table[code], base)
         return base
 
-    for t in range(tiles):
-        for f in (0, 2):
+    def joined(f):
+        for t in range(tiles):
             merged = jnp.where(tip, halo[:, f // 2, 0, t], halo[:, f // 2, 1, t])
             x[:, f, t, :, main:] = jnp.where(real, merged, 0.0)
+
+    joined(0)
+    for t in range(tiles):
         merged = classed(jnp.where(tip, halo_fac[:, 0, t], halo_fac[:, 1, t]))
         x[:, 1, t, :, main:] = jnp.where(real, merged, 0.0)
         x[:, 1, t, :, :main] = classed(fac[:, t, :, :main])
@@ -239,6 +250,8 @@
             for side in range(2):
                 rim_ans[side, 1] = jnp.where(inside[side], rims[side, :, 0], 0.0)
                 rim_base[side] = jnp.where(inside[side], rims[side, :, 1], 0.0)
+            dealt(2)
+            joined(2)
 
         rim_p = [rim_ans[side, 1] for side in range(2)]
         rim_m = [mobility(rim_base[side], rim_p[side]) for side in range(2)]

time: 65.8 us -> 65.1 us (0.989)
  Pallas kernels: 62.2 us -> 61.5 us
    pallas_call x1, Pallas kernels: 62.2 us -> 61.5 us  [per_device(): pl.pallas_call(functools.partial(kernel, crosses, strikes, rows * strikes...]
where the time goes in v5:
time: 65.1 us; the launch traced here: 64.9 us
  Pallas kernels  61.5 us (94%)
  local copies, waits for them, and re-layouts  2.72 us (4%)
    pallas_call x1, Pallas kernels, per_device(): pl.pallas_call(functools.partial(kernel, crosses, strikes, rows * strikes...  61.5 us
    unnamed x4, local copies, waits for them, and re-layouts  2.72 us

profile of v5, /device:TPU:0, one launch (start us, length us, event | category | flops | bytes accessed | tf_op | source)
XLA Modules:
  0.0 64.9 jit_solution(1090644910234655670)
XLA Ops:
  0.6 61.5 %shard_map.59 = (f32[8,8,1,2048]{3,2,1,0:T(1,128)}, f32[8,8,1,2048]{3,2,1,0:T(1,128)}) custom-call(f32[8,8,1,2048]{3,2,1,0:T(1,128)} %bitcast.5, s32[8,8,1,2048]{3,2,1,0:T(1,128)} %bitcast.6, f32[8,8,1,2048]{3,2,1,0:T(1,128)} %bitcast.7, f32[8]{0:T(128)} %table.1), custom_call_target="tpu_custom_call" | custom-call | tf_op jit(solution)/shard_map/pallas_call | solution.py:458
  62.2 0.0 copy-start
  62.2 1.9 %copy.8 = f32[64,1,2048]{2,1,0:T(1,128)} copy(f32[64,1,2048]{2,1,0:T(1,128)} %bitcast.9) | data formatting | bytes 1048576
  64.1 0.0 copy-done
  64.1 0.8 %copy.9 = f32[64,1,2048]{2,1,0:T(1,128)} copy(f32[64,1,2048]{2,1,0:T(1,128)S(1)} %bitcast.8) | data formatting | bytes 1048576
Async XLA Ops:
  62.2 1.9 %copy-start = (f32[8,8,1,2048]{3,2,1,0:T(1,128)S(1)}, f32[8,8,1,2048]{3,2,1,0:T(1,128)}, u32[]{:S(2)}) copy-start(f32[8,8,1,2048]{3,2,1,0:T(1,128)} %get-tuple-element.5) | copy-start | bytes 1572868

commit v6 on v5

--- a/solution.py
+++ b/solution.py
@@ -172,12 +172,12 @@
     for copy in rim_copies:
         copy.start()
 
-    def finals(which):
+    def finals(which, blocks):
         ref = out_p if which == 0 else out_d
         copies = []
-        for k in range(crosses):
+        for k in reversed(range(crosses)):
             to = across(k)
-            for t in range(tiles):
+            for t in blocks:
                 src = x.at[to, 0, t] if which == 0 else res.at[to, t]
                 copies.append(
                     send(
@@ -279,7 +279,7 @@
 
         @pl.when(step == DEFECT - 1)
         def _():
-            for copy in finals(1):
+            for copy in finals(1, range(tiles)):
                 copy.start()
 
         finish()
@@ -409,14 +409,18 @@
         lax.fori_loop(0, SWEEPS, sweep, 0)
         for t in range(tiles):
             x[:, 0, t] = x[:, 0, t] + ans[t]
+
+            @pl.when(step == DEFECT - 1)
+            def _(t=t):
+                for copy in finals(0, [t]):
+                    copy.start()
+
         for side in range(2):
             rim_ans[side, 1] = rim_ans[side, 1] + jnp.where(inside[side], rim_ans[side, 0], 0.0)
         return carry
 
     lax.fori_loop(0, DEFECT, one_step, 0)
 
-    for copy in finals(0):
-        copy.start()
     for which in (1, 0):
         ref = out_p if which == 0 else out_d
         for k in range(crosses):

time: 65.1 us -> 65.3 us (level)
  no operation moved by 1% of the time
where the time goes in v6:
time: 65.3 us; the launch traced here: 65.1 us
  Pallas kernels  61.8 us (95%)
  local copies, waits for them, and re-layouts  2.72 us (4%)
    pallas_call x1, Pallas kernels, per_device(): pl.pallas_call(functools.partial(kernel, crosses, strikes, rows * strikes...  61.8 us
    unnamed x4, local copies, waits for them, and re-layouts  2.72 us

profile of v6, /device:TPU:0, one launch (start us, length us, event | category | flops | bytes accessed | tf_op | source)
XLA Modules:
  0.0 65.1 jit_solution(4244400108135441009)
XLA Ops:
  0.6 61.8 %shard_map.59 = (f32[8,8,1,2048]{3,2,1,0:T(1,128)}, f32[8,8,1,2048]{3,2,1,0:T(1,128)}) custom-call(f32[8,8,1,2048]{3,2,1,0:T(1,128)} %bitcast.5, s32[8,8,1,2048]{3,2,1,0:T(1,128)} %bitcast.6, f32[8,8,1,2048]{3,2,1,0:T(1,128)} %bitcast.7, f32[8]{0:T(128)} %table.1), custom_call_target="tpu_custom_call" | custom-call | tf_op jit(solution)/shard_map/pallas_call | solution.py:462
  62.4 0.0 copy-start
  62.4 1.9 %copy.8 = f32[64,1,2048]{2,1,0:T(1,128)} copy(f32[64,1,2048]{2,1,0:T(1,128)} %bitcast.9) | data formatting | bytes 1048576
  64.3 0.0 copy-done
  64.3 0.8 %copy.9 = f32[64,1,2048]{2,1,0:T(1,128)} copy(f32[64,1,2048]{2,1,0:T(1,128)S(1)} %bitcast.8) | data formatting | bytes 1048576
Async XLA Ops:
  62.4 1.9 %copy-start = (f32[8,8,1,2048]{3,2,1,0:T(1,128)S(1)}, f32[8,8,1,2048]{3,2,1,0:T(1,128)}, u32[]{:S(2)}) copy-start(f32[8,8,1,2048]{3,2,1,0:T(1,128)} %get-tuple-element.5) | copy-start | bytes 1572868

commit v7 on v5

--- a/solution.py
+++ b/solution.py
@@ -175,7 +175,7 @@
     def finals(which):
         ref = out_p if which == 0 else out_d
         copies = []
-        for k in range(crosses):
+        for k in reversed(range(crosses)):
             to = across(k)
             for t in range(tiles):
                 src = x.at[to, 0, t] if which == 0 else res.at[to, t]

time: 65.1 us -> 65 us (level)
  no operation moved by 1% of the time
where the time goes in v7:
time: 65 us; the launch traced here: 64.9 us
  Pallas kernels  61.5 us (95%)
  local copies, waits for them, and re-layouts  2.72 us (4%)
  between operations  0.65 us (1%)
    pallas_call x1, Pallas kernels, per_device(): pl.pallas_call(functools.partial(kernel, crosses, strikes, rows * strikes...  61.5 us
    unnamed x4, local copies, waits for them, and re-layouts  2.72 us

profile of v7, /device:TPU:0, one launch (start us, length us, event | category | flops | bytes accessed | tf_op | source)
XLA Modules:
  0.0 64.9 jit_solution(18433259673363038668)
XLA Ops:
  0.6 61.5 %shard_map.59 = (f32[8,8,1,2048]{3,2,1,0:T(1,128)}, f32[8,8,1,2048]{3,2,1,0:T(1,128)}) custom-call(f32[8,8,1,2048]{3,2,1,0:T(1,128)} %bitcast.5, s32[8,8,1,2048]{3,2,1,0:T(1,128)} %bitcast.6, f32[8,8,1,2048]{3,2,1,0:T(1,128)} %bitcast.7, f32[8]{0:T(128)} %table.1), custom_call_target="tpu_custom_call" | custom-call | tf_op jit(solution)/shard_map/pallas_call | solution.py:458
  62.1 0.0 copy-start
  62.1 1.9 %copy.8 = f32[64,1,2048]{2,1,0:T(1,128)} copy(f32[64,1,2048]{2,1,0:T(1,128)} %bitcast.9) | data formatting | bytes 1048576
  64.1 0.0 copy-done
  64.1 0.8 %copy.9 = f32[64,1,2048]{2,1,0:T(1,128)} copy(f32[64,1,2048]{2,1,0:T(1,128)S(1)} %bitcast.8) | data formatting | bytes 1048576
Async XLA Ops:
  62.1 1.9 %copy-start = (f32[8,8,1,2048]{3,2,1,0:T(1,128)S(1)}, f32[8,8,1,2048]{3,2,1,0:T(1,128)}, u32[]{:S(2)}) copy-start(f32[8,8,1,2048]{3,2,1,0:T(1,128)} %get-tuple-element.5) | copy-start | bytes 1572868
